TPU v7x, 32 devices: a whole 2x2x4 slice. The times are simulated.
32 devices in a mesh: batch: 4 (over x, core), mp: 8 (over z, y).
Axes of the slice: x: 2, y: 2, z: 4, core: 2. Of those that a mesh axis runs over, the one named last changes fastest.
Arguments:
- features: bfloat16 [256, 8192], P('mp', 'batch'), may hold values from -5 to 5
- counts: int32 [4], P('batch'), may hold values from 16 to 32, as said below
- labels: int32 [128], P('batch'), may hold values from 0 to 99
- teacher: float32 [128, 100], P('batch'), may hold values from -30 to 30
- conv1_weight: bfloat16 [256, 9, 256], P('mp'), may hold values from -0.125 to 0.125
- bn1_gain: float32 [256], P('mp'), may hold values from 0.5 to 1.5
- bn1_bias: float32 [256], P('mp'), may hold values from -3 to 3
- conv2_weight: bfloat16 [256, 9, 256], P('mp'), may hold values from -0.125 to 0.125
- bn2_gain: float32 [256], P('mp'), may hold values from 0.5 to 1.5
- bn2_bias: float32 [256], P('mp'), may hold values from -3 to 3
- head_weight: bfloat16 [256, 100], P('mp'), may hold values from -3 to 3
- head_bias: float32 [100], replicated, may hold values from -4 to 4
- run_mean1: float32 [256], P('mp'), may hold values from -3 to 3
- run_var1: float32 [256], P('mp'), may hold values from 0.5 to 2
- run_mean2: float32 [256], P('mp'), may hold values from -3 to 3
- run_var2: float32 [256], P('mp'), may hold values from 0.5 to 2
Outputs:
- loss: float32 [], replicated
- grad_features: float32 [256, 8192], P('mp', 'batch')
- grad_conv1: float32 [256, 9, 256], P('mp')
- grad_gain1: float32 [256], P('mp')
- grad_bias1: float32 [256], P('mp')
- grad_conv2: float32 [256, 9, 256], P('mp')
- grad_gain2: float32 [256], P('mp')
- grad_bias2: float32 [256], P('mp')
- grad_head: float32 [256, 100], P('mp')
- grad_head_bias: float32 [100], replicated
- new_mean1: float32 [256], P('mp')
- new_var1: float32 [256], P('mp')
- new_mean2: float32 [256], P('mp')
- new_var2: float32 [256], P('mp')
Inputs may be any that keep to these rules, and one draw needn't show every extreme that they name: counts[b] live images stand first among the 32 slots of batch index b; some index holds 32 live images in every draw.
All inputs are finite; a program needn't handle non-finite values.
Results may differ from a plain program's by a relative error of at most 0.0048.
Values may be sent and summed in bfloat16 or wider, within the bound.
A program may use at most 128 MiB of HBM per device.

v0:
```python
import jax
import jax.numpy as jnp
from jax import lax
from jax.sharding import PartitionSpec as P

SIDE = 8


epsilon = 1e-05
softening_heat = 4.0
target_weight = 1.0
other_weight = 8.0
loss_scale = 1024.0
momentum = 0.1
highest = lax.Precision.HIGHEST


def shifted_taps(field, sign):
    channels = field.shape[0]
    planes = field.reshape(channels, -1, SIDE, SIDE)
    padded = jnp.pad(planes, ((0, 0), (0, 0), (1, 1), (1, 1)))
    pieces = []
    for vertical in range(3):
        for lateral in range(3):
            row_start = 1 + sign * (vertical - 1)
            col_start = 1 + sign * (lateral - 1)
            pieces.append(
                padded[:, :, row_start : row_start + SIDE, col_start : col_start + SIDE].reshape(
                    channels, -1
                )
            )
    return jnp.stack(pieces)


def image_losses(class_logits, teacher, labels):
    onehot = (labels[:, None] == jnp.arange(class_logits.shape[1])[None, :]).astype(
        class_logits.dtype
    )
    cross = jax.nn.logsumexp(class_logits, axis=1) - jnp.sum(onehot * class_logits, axis=1)
    pupil_network = class_logits / softening_heat
    mentor_network = teacher / softening_heat
    student_rest = pupil_network - 1000.0 * onehot
    tutor_rest = mentor_network - 1000.0 * onehot
    student_all = jax.nn.logsumexp(pupil_network, axis=1)
    tutor_all = jax.nn.logsumexp(mentor_network, axis=1)
    student_other = jax.nn.logsumexp(student_rest, axis=1)
    tutor_other = jax.nn.logsumexp(tutor_rest, axis=1)
    student_hit = jnp.sum(onehot * pupil_network, axis=1) - student_all
    tutor_hit = jnp.sum(onehot * mentor_network, axis=1) - tutor_all
    student_miss = student_other - student_all
    tutor_miss = tutor_other - tutor_all
    binary = jnp.exp(tutor_hit) * (tutor_hit - student_hit) + jnp.exp(tutor_miss) * (
        tutor_miss - student_miss
    )
    tutor_log = tutor_rest - tutor_other[:, None]
    student_log = student_rest - student_other[:, None]
    spread = jnp.sum(jnp.exp(tutor_log) * (tutor_log - student_log), axis=1)
    squared_value = softening_heat * softening_heat
    return cross + squared_value * (target_weight * binary + other_weight * spread)


def silu_slope(values):
    sigma = jax.nn.sigmoid(values)
    return sigma * (1.0 + values * (1.0 - sigma))


def conv_piece(weight, piece):
    return jnp.einsum(
        "otc,tcn->on", weight, shifted_taps(piece, 1), preferred_element_type=jnp.float32
    )


def weight_piece(grad_low, piece):
    return jnp.einsum(
        "on,tcn->otc", grad_low, shifted_taps(piece, 1), preferred_element_type=jnp.float32
    )


def input_piece(weight, back_taps):
    return jnp.einsum("otc,ton->cn", weight, back_taps, preferred_element_type=jnp.float32)


def per_device(
    features,
    counts,
    labels,
    teacher,
    conv1_weight,
    bn1_gain,
    bn1_bias,
    conv2_weight,
    bn2_gain,
    bn2_bias,
    head_weight,
    head_bias,
    run_mean1,
    run_var1,
    run_mean2,
    run_var2,
):
    channels, cell_count = features.shape
    image_area = SIDE * SIDE
    image_slots = cell_count // image_area
    image_present = (lax.broadcasted_iota(jnp.int32, (image_slots,), 0) < counts[0]).astype(
        jnp.float32
    )
    cell_live = jnp.broadcast_to(image_present[:, None], (image_slots, image_area)).reshape(-1)
    residual_in = features.astype(jnp.float32)
    first = conv_piece(conv1_weight, lax.all_gather(features, "mp", axis=0, tiled=True))
    first_sum, first_square, cells = lax.psum(
        (
            jnp.sum(first * cell_live[None, :], axis=1),
            jnp.sum(first * first * cell_live[None, :], axis=1),
            jnp.sum(cell_live),
        ),
        "batch",
    )
    mean1 = first_sum / cells
    var1 = first_square / cells - mean1 * mean1
    rstd1 = lax.rsqrt(var1 + epsilon)
    normed1 = (first - mean1[:, None]) * rstd1[:, None]
    pre1 = bn1_gain[:, None] * normed1 + bn1_bias[:, None]
    hidden = jax.nn.silu(pre1).astype(jnp.bfloat16)
    second = conv_piece(conv2_weight, lax.all_gather(hidden, "mp", axis=0, tiled=True))
    second_sum, second_square = lax.psum(
        (
            jnp.sum(second * cell_live[None, :], axis=1),
            jnp.sum(second * second * cell_live[None, :], axis=1),
        ),
        "batch",
    )
    mean2 = second_sum / cells
    var2 = second_square / cells - mean2 * mean2
    rstd2 = lax.rsqrt(var2 + epsilon)
    normed2 = (second - mean2[:, None]) * rstd2[:, None]
    pre2 = bn2_gain[:, None] * normed2 + bn2_bias[:, None] + residual_in
    block_out = jax.nn.silu(pre2)
    pooled = jnp.mean(block_out.reshape(channels, image_slots, image_area), axis=2)
    head_local = head_weight.astype(jnp.float32)
    partial_logits = jnp.einsum("cm,ck->mk", pooled, head_local, precision=highest)
    class_logits = lax.psum(partial_logits, "mp") + head_bias[None, :]
    image_batch = cells / image_area

    def losses_of(values):
        return image_losses(values, teacher, labels)

    per_image, pullback = jax.vjp(losses_of, class_logits)
    loss_part = jnp.sum(image_present * per_image)
    (grad_logits,) = pullback(image_present * (loss_scale / image_batch))
    head_grad = jnp.einsum("cm,mk->ck", pooled, grad_logits, precision=highest)
    head_bias_grad = jnp.sum(grad_logits, axis=0)
    grad_pooled = jnp.einsum("mk,ck->cm", grad_logits, head_local, precision=highest) / image_area
    grad_out = jnp.broadcast_to(
        grad_pooled[:, :, None], (channels, image_slots, image_area)
    ).reshape(channels, -1)
    grad_pre2 = grad_out * silu_slope(pre2)
    loss_total = lax.psum(loss_part, "batch")
    bias2_grad, gain2_grad = lax.psum(
        (jnp.sum(grad_pre2, axis=1), jnp.sum(grad_pre2 * normed2, axis=1)), "batch"
    )
    loss = loss_total / image_batch
    grad_second = (bn2_gain * rstd2)[:, None] * (
        grad_pre2
        - cell_live[None, :] * (bias2_grad[:, None] + normed2 * gain2_grad[:, None]) / cells
    )
    second_low = grad_second.astype(jnp.bfloat16)
    conv2_grad = weight_piece(second_low, lax.all_gather(hidden, "mp", axis=0, tiled=True))
    back_second = shifted_taps(second_low, -1)
    grad_hidden = lax.psum_scatter(
        input_piece(conv2_weight, back_second), "mp", scatter_dimension=0, tiled=True
    )
    grad_pre1 = grad_hidden * silu_slope(pre1)
    bias1_grad, gain1_grad = lax.psum(
        (jnp.sum(grad_pre1, axis=1), jnp.sum(grad_pre1 * normed1, axis=1)), "batch"
    )
    grad_first = (bn1_gain * rstd1)[:, None] * (
        grad_pre1
        - cell_live[None, :] * (bias1_grad[:, None] + normed1 * gain1_grad[:, None]) / cells
    )
    first_low = grad_first.astype(jnp.bfloat16)
    conv1_grad = weight_piece(first_low, lax.all_gather(features, "mp", axis=0, tiled=True))
    back_first = shifted_taps(first_low, -1)
    input_term = lax.psum_scatter(
        input_piece(conv1_weight, back_first), "mp", scatter_dimension=0, tiled=True
    )
    grad_features = input_term + grad_pre2
    conv1_grad, conv2_grad, head_grad, head_bias_grad = lax.psum(
        (conv1_grad, conv2_grad, head_grad, head_bias_grad), "batch"
    )
    bias_adjustment = cells / (cells - 1.0)
    new_mean1 = (1.0 - momentum) * run_mean1 + momentum * mean1
    new_var1 = (1.0 - momentum) * run_var1 + momentum * var1 * bias_adjustment
    new_mean2 = (1.0 - momentum) * run_mean2 + momentum * mean2
    new_var2 = (1.0 - momentum) * run_var2 + momentum * var2 * bias_adjustment
    return (
        loss,
        grad_features,
        conv1_grad,
        gain1_grad,
        bias1_grad,
        conv2_grad,
        gain2_grad,
        bias2_grad,
        head_grad,
        head_bias_grad,
        new_mean1,
        new_var1,
        new_mean2,
        new_var2,
    )


def solution(mesh):
    return jax.shard_map(
        per_device,
        mesh=mesh,
        in_specs=(
            P("mp", "batch"),
            P("batch"),
            P("batch"),
            P("batch", None),
            P("mp", None, None),
            P("mp"),
            P("mp"),
            P("mp", None, None),
            P("mp"),
            P("mp"),
            P("mp", None),
            P(),
            P("mp"),
            P("mp"),
            P("mp"),
            P("mp"),
        ),
        out_specs=(
            P(),
            P("mp", "batch"),
            P("mp", None, None),
            P("mp"),
            P("mp"),
            P("mp", None, None),
            P("mp"),
            P("mp"),
            P("mp", None),
            P(),
            P("mp"),
            P("mp"),
            P("mp"),
            P("mp"),
        ),
        check_vma=False,
    )
```

profile of v0, /device:TPU:0, one launch (start us, length us, event | category | flops | bytes accessed | tf_op | source)
XLA Modules:
  0.0 470.6 jit_solution(7038195619876335994)
XLA Ops:
  10.0 43.0 %all-gather.3.cloned.1.call-done = bf16[256,2048]{1,0:T(8,128)(2,1)} async-done(((bf16[32,2048]{1,0:T(8,128)(2,1)}), bf16[256,2048]{1,0:T(8,128)(2,1)}) %all-gather.3.cloned.1.call-update) | async-done | bytes 1048592 | tf_op jit(solution)/shard_map/all_gather | solution.py:109
  53.0 2.3 copy.72
  55.3 6.2 %pad_slice_fusion.8 = (bf16[256,32,8,8]{0,3,2,1:T(8,128)(2,1)S(1)}, bf16[256,32,8,8]{0,3,2,1:T(8,128)(2,1)}, bf16[256,32,8,8]{0,3,2,1:T(8,128)(2,1)}, bf16[256,3...) fusion(bf16[256,32,8,8]{0,3,2,1:T(8,128)(2,1)} %bitcast.150), kind=kLoop, calls=%fused_computation.8 | loop fusion | bytes 9437184 | tf_op jit(solution)/shard_map/slice | solution.py:28
  61.5 2.3 copy.73
  63.8 2.3 constant_dynamic-update-slice_fusion.7
  66.1 2.3 copy.74
  68.4 2.3 copy.75
  70.6 2.3 copy.76
  72.9 2.3 copy.77
  75.2 1.4 copy.78
  78.0 2.5 constant_dynamic-update-slice_fusion.6
  88.1 5.6 %multiply_reduce_fusion.3 = (f32[32]{0:T(128)S(1)}, f32[32]{0:T(128)S(1)}, f32[2048,32]{0,1:T(8,128)S(1)}) fusion(f32[2048]{0:T(1024)S(1)} %copy-done.16, bf16[32,9,256]{2,0,1:T(8,128)(2,1)S(1)} %copy-done.12, bf16[9,256,2048]{2,1,0:T(8,128)(2,1)} %constant_dynamic-update-slice_fusion), kind=kOutput, calls=%fused_computation.72 | convolution fusion | flops 302317504 | bytes 9855232 | tf_op jit(solution)/shard_map/otc,tcn->on/dot_general | solution.py:68
  93.6 6.3 %all-reduce.7 = (f32[]{:T(128)}, f32[32]{0:T(128)S(1)}, f32[32]{0:T(128)S(1)}) all-reduce(f32[]{:T(128)} %broadcast_reduce_fusion, f32[32]{0:T(128)S(1)} %get-tuple-element.17, f32[32]{0:T(128)S(1)} %get-tuple-element.16), channel_id=1, replica_groups=mesh['batch'=4,'mp'=8] {'batch'}, use_global_device_ids=true, to_apply=%region_3.4 | all-reduce | flops 65 | bytes 520 | tf_op jit(solution)/shard_map/psum | solution.py:110
  106.3 36.8 %all-gather.5.cloned.1.call-done = bf16[256,2048]{1,0:T(8,128)(2,1)} async-done(((bf16[32,2048]{1,0:T(8,128)(2,1)}), bf16[256,2048]{1,0:T(8,128)(2,1)}) %all-gather.5.cloned.1.call-update) | async-done | bytes 1048592 | tf_op jit(solution)/shard_map/all_gather | solution.py:124
  143.1 2.3 copy.81
  145.4 6.1 %pad_slice_fusion = (bf16[256,32,8,8]{0,3,2,1:T(8,128)(2,1)S(1)}, bf16[256,32,8,8]{0,3,2,1:T(8,128)(2,1)}, bf16[256,32,8,8]{0,3,2,1:T(8,128)(2,1)}, bf16[256,32,...) fusion(bf16[256,32,8,8]{0,3,2,1:T(8,128)(2,1)} %bitcast.151), kind=kLoop, calls=%fused_computation | loop fusion | bytes 9437184 | tf_op jit(solution)/shard_map/slice | solution.py:28
  151.5 2.3 copy.82
  153.8 2.3 constant_dynamic-update-slice_fusion.15
  156.1 2.3 copy.83
  158.4 2.3 copy.84
  160.7 2.3 copy.85
  163.0 2.3 copy.86
  165.3 1.4 copy.87
  168.0 2.5 constant_dynamic-update-slice_fusion.14
  178.1 5.6 %multiply_reduce_fusion.1 = (f32[32]{0:T(128)S(1)}, f32[32]{0:T(128)S(1)}, f32[2048,32]{0,1:T(8,128)S(1)}) fusion(f32[2048]{0:T(1024)S(1)} %copy-done.17, bf16[32,9,256]{2,0,1:T(8,128)(2,1)S(1)} %copy-done, bf16[9,256,2048]{2,1,0:T(8,128)(2,1)} %constant_dynamic-update-slice_fusion.8), kind=kOutput, calls=%fused_computation.67 | convolution fusion | flops 302317504 | bytes 9855232 | tf_op jit(solution)/shard_map/otc,tcn->on/dot_general | solution.py:68
  183.8 5.8 %all-reduce.6 = (f32[32]{0:T(128)S(1)}, f32[32]{0:T(128)S(1)}) all-reduce(f32[32]{0:T(128)S(1)} %get-tuple-element.15, f32[32]{0:T(128)S(1)} %get-tuple-element.14), channel_id=1, replica_groups=mesh['batch'=4,'mp'=8] {'batch'}, use_global_device_ids=true, to_apply=%region_9.10 | all-reduce | flops 64 | bytes 512 | tf_op jit(solution)/shard_map/psum | solution.py:125
  191.6 34.9 %psum.110 = f32[32,100]{1,0:T(8,128)S(1)} all-reduce(f32[32,100]{1,0:T(8,128)S(1)} %fusion.25), channel_id=1, replica_groups=mesh['batch'=4,'mp'=8] {'mp'}, use_global_device_ids=true, to_apply=%region_11.12 | all-reduce | flops 3200 | bytes 25600 | tf_op jit(solution)/shard_map/psum | solution.py:141
  229.3 5.7 %all-reduce.5 = (f32[32]{0:T(128)S(1)}, f32[32]{0:T(128)S(1)}) all-reduce(f32[32]{0:T(128)S(1)} %get-tuple-element.21, f32[32]{0:T(128)S(1)} %get-tuple-element.20), channel_id=1, replica_groups=mesh['batch'=4,'mp'=8] {'batch'}, use_global_device_ids=true, to_apply=%region_32.33 | all-reduce | flops 64 | bytes 512 | tf_op jit(solution)/shard_map/psum | solution.py:158
  236.8 5.5 %pad_slice_fusion.24 = (bf16[32,32,8,8]{0,3,2,1:T(8,128)(2,1)S(1)}, bf16[32,32,8,8]{0,3,2,1:T(8,128)(2,1)}, bf16[32,32,8,8]{0,3,2,1:T(8,128)(2,1)}, bf16[32,32,8...) fusion(bf16[32,32,8,8]{0,3,2,1:T(8,128)(2,1)} %bitcast.168), kind=kLoop, calls=%fused_computation.24 | loop fusion | bytes 1179648 | tf_op jit(solution)/shard_map/slice | solution.py:28
  242.3 1.2 copy.92
  244.2 1.2 copy.93
  245.4 1.2 copy.94
  246.6 1.2 copy.95
  253.9 3.4 convolution_bitcast_fusion.1
  257.5 65.4 %reduce-scatter.3.cloned.1.call-done = f32[32,2048]{1,0:T(8,128)} async-done(((f32[256,2048]{1,0:T(8,128)}), f32[32,2048]{1,0:T(8,128)}) %reduce-scatter.3.cloned.1.call-update) | async-done | bytes 262160 | tf_op jit(solution)/shard_map/reduce_scatter | solution.py:169
  322.9 1.3 fusion.47
  324.2 11.4 %all-reduce.4 = (f32[]{:T(128)}, f32[32]{0:T(128)S(1)}, f32[32]{0:T(128)S(1)}, f32[32,100]{1,0:T(8,128)}, f32[100]{0:T(128)}) all-reduce(f32[]{:T(128)} %get-tuple-element.96, f32[32]{0:T(128)S(1)} %get-tuple-element.19, f32[32]{0:T(128)S(1)} %get-tuple-element.18, ...), channel_id=1, replica_groups=mesh['batch'=4,'mp'=8] {'batch'}, use_global_device_ids=true, to_apply=%region_27.28 | all-reduce | flops 3365 | bytes 26920 | tf_op jit(solution)/shard_map/psum | solution.py:157
  337.4 5.0 %pad_slice_fusion.16 = (bf16[32,32,8,8]{0,3,2,1:T(8,128)(2,1)S(1)}, bf16[32,32,8,8]{0,3,2,1:T(8,128)(2,1)}, bf16[32,32,8,8]{0,3,2,1:T(8,128)(2,1)}, bf16[32,32,8...) fusion(bf16[32,32,8,8]{0,3,2,1:T(8,128)(2,1)} %bitcast.169), kind=kLoop, calls=%fused_computation.16 | loop fusion | bytes 1179648 | tf_op jit(solution)/shard_map/slice | solution.py:28
  345.5 1.9 copy.104
  348.3 1.6 constant_dynamic-update-slice_fusion.29
  354.5 3.3 convolution_bitcast_fusion
  358.2 7.3 %fusion.19 = f32[32,9,256]{2,0,1:T(8,128)} fusion(bf16[9,256,2048]{2,1,0:T(8,128)(2,1)} %constant_dynamic-update-slice_fusion.8, bf16[32,2048]{1,0:T(8,128)(2,1)S(1)} %fusion.18), kind=kOutput, calls=%fused_computation.75 | convolution fusion | flops 301989888 | bytes 9863168 | tf_op jit(solution)/shard_map/on,tcn->otc/dot_general | solution.py:74
  365.5 7.3 %fusion.21 = f32[32,9,256]{2,0,1:T(8,128)} fusion(bf16[9,256,2048]{2,1,0:T(8,128)(2,1)} %constant_dynamic-update-slice_fusion, bf16[32,2048]{1,0:T(8,128)(2,1)S(1)} %fusion.17), kind=kOutput, calls=%fused_computation.77 | convolution fusion | flops 301989888 | bytes 9863168 | tf_op jit(solution)/shard_map/on,tcn->otc/dot_general | solution.py:74
  374.5 49.6 %reduce-scatter.5.cloned.1.call-done = f32[32,2048]{1,0:T(8,128)} async-done(((f32[256,2048]{1,0:T(8,128)}), f32[32,2048]{1,0:T(8,128)}) %reduce-scatter.5.cloned.1.call-update) | async-done | bytes 262160 | tf_op jit(solution)/shard_map/reduce_scatter | solution.py:183
  424.1 1.7 add.179
  425.8 33.7 %all-reduce.11.cloned.1.call-done = (f32[32,9,256]{2,0,1:T(8,128)}, f32[32,9,256]{2,0,1:T(8,128)}) async-done(((f32[32,9,256]{2,0,1:T(8,128)}, f32[32,9,256]{2,0,1:T(8,128)}), (f32[32,9,256]{2,0,1:T(8,128)}, f32[32,9,256]{2,0,1:T(8,128)})) %all-reduce.11.cloned.1.call-update) | async-done | bytes 589840 | tf_op jit(solution)/shard_map/psum | solution.py:187
  459.5 1.7 copy.150
  461.2 1.7 copy.151
  (200 shorter events, 49.2 us)
Async XLA Ops:
  7.2 170.8 %copy-start = (bf16[32,9,256]{2,0,1:T(8,128)(2,1)S(1)}, bf16[32,9,256]{2,0,1:T(8,128)(2,1)}, u32[]{:S(2)}) copy-start(bf16[32,9,256]{2,0,1:T(8,128)(2,1)} %param.23) | copy-start | bytes 442372
  7.2 45.8 %all-gather.3.cloned.1.call-start = ((), (), s32[]{:S(2)}) async-start(), calls=%async_computation.2 | async-start | bytes 1179648 | tf_op jit(solution)/shard_map/all_gather | solution.py:109
  7.9 135.2 %all-gather.5.cloned.1.call-start = ((), (), s32[]{:S(2)}) async-start(), calls=%async_computation.3 | async-start | bytes 1179648 | tf_op jit(solution)/shard_map/all_gather | solution.py:124
  78.0 2.5 copy-start.9
  78.0 3.6 copy-start.7
  85.8 2.2 copy-start.12
  85.8 2.2 copy-start.16
  88.0 13.2 %copy-start.44 = (f32[32]{0:T(128)S(1)}, f32[32]{0:T(128)}, u32[]{:S(2)}) copy-start(f32[32]{0:T(128)} %param.29) | copy-start | bytes 388
  88.0 14.4 %copy-start.31 = (f32[32]{0:T(128)S(1)}, f32[32]{0:T(128)}, u32[]{:S(2)}) copy-start(f32[32]{0:T(128)} %param.21) | copy-start | bytes 388
  88.0 14.9 %copy-start.36 = (f32[32]{0:T(128)S(1)}, f32[32]{0:T(128)}, u32[]{:S(2)}) copy-start(f32[32]{0:T(128)} %param.22) | copy-start | bytes 388
  88.0 15.8 %copy-start.14 = (f32[32,100]{1,0:T(8,128)S(1)}, f32[32,100]{1,0:T(8,128)}, u32[]{:S(2)}) copy-start(f32[32,100]{1,0:T(8,128)} %param.19) | copy-start | bytes 38404
  88.0 15.8 %copy-start.20 = (s32[32]{0:T(128)S(1)}, s32[32]{0:T(128)}, u32[]{:S(2)}) copy-start(s32[32]{0:T(128)} %param.18) | copy-start | bytes 388
  102.4 42.9 %copy-start.25 = (f32[32]{0:T(128)}, f32[32]{0:T(128)S(1)}, u32[]{:S(2)}) copy-start(f32[32]{0:T(128)S(1)} %get-tuple-element.53) | copy-start | bytes 388
  102.9 42.4 %copy-start.23 = (f32[32]{0:T(128)}, f32[32]{0:T(128)S(1)}, u32[]{:S(2)}) copy-start(f32[32]{0:T(128)S(1)} %get-tuple-element.99) | copy-start | bytes 388
  103.8 219.1 %reduce-scatter.3.cloned.1.call-start = ((), (), s32[]{:S(2)}) async-start(), calls=%async_computation.4 | async-start | bytes 2359296 | tf_op jit(solution)/shard_map/reduce_scatter | solution.py:169
  104.0 41.3 %copy-start.40 = (f32[32]{0:T(128)}, f32[32]{0:T(128)S(1)}, u32[]{:S(2)}) copy-start(f32[32]{0:T(128)S(1)} %fusion.46) | copy-start | bytes 388
  105.8 39.6 %copy-start.33 = (f32[32]{0:T(128)}, f32[32]{0:T(128)S(1)}, u32[]{:S(2)}) copy-start(f32[32]{0:T(128)S(1)} %get-tuple-element.61) | copy-start | bytes 388
  168.0 2.5 copy-start.10
  168.0 3.5 copy-start.8
  175.8 2.2 copy-start.17
  178.0 11.6 %copy-start.45 = (f32[32]{0:T(128)S(1)}, f32[32]{0:T(128)}, u32[]{:S(2)}) copy-start(f32[32]{0:T(128)} %param.31) | copy-start | bytes 388
  178.0 12.8 %copy-start.30 = (f32[32]{0:T(128)S(1)}, f32[32]{0:T(128)}, u32[]{:S(2)}) copy-start(f32[32]{0:T(128)} %param.24) | copy-start | bytes 388
  178.0 12.8 %copy-start.11 = (bf16[32,2048]{1,0:T(8,128)(2,1)S(1)}, bf16[32,2048]{1,0:T(8,128)(2,1)}, u32[]{:S(2)}) copy-start(bf16[32,2048]{1,0:T(8,128)(2,1)} %param.16) | copy-start | bytes 393220
  178.0 12.8 %copy-start.35 = (f32[32]{0:T(128)S(1)}, f32[32]{0:T(128)}, u32[]{:S(2)}) copy-start(f32[32]{0:T(128)} %param.25) | copy-start | bytes 388
  178.0 13.4 %copy-start.19 = (bf16[32,100]{1,0:T(8,128)(2,1)S(1)}, bf16[32,100]{1,0:T(8,128)(2,1)}, u32[]{:S(2)}) copy-start(bf16[32,100]{1,0:T(8,128)(2,1)} %param.26) | copy-start | bytes 19204
  178.0 48.5 %copy-start.15 = (f32[32,100]{1,0:T(8,128)S(1)}, f32[32,100]{1,0:T(8,128)}, u32[]{:S(2)}) copy-start(f32[32,100]{1,0:T(8,128)} %param.19) | copy-start | bytes 38404
  178.1 48.5 %copy-start.21 = (s32[32]{0:T(128)S(1)}, s32[32]{0:T(128)}, u32[]{:S(2)}) copy-start(s32[32]{0:T(128)} %param.18) | copy-start | bytes 388
  178.1 48.5 %copy-start.22 = (f32[100]{0:T(128)S(1)}, f32[100]{0:T(128)}, u32[]{:S(2)}) copy-start(f32[100]{0:T(128)} %param.27) | copy-start | bytes 1204
  178.1 48.5 %copy-start.43 = (f32[32]{0:T(128)S(1)}, f32[32]{0:T(128)}, u32[]{:S(2)}) copy-start(f32[32]{0:T(128)} %is-finite_select_fusion.1) | copy-start | bytes 388
  178.1 48.9 %copy-start.41 = (f32[32]{0:T(128)S(1)}, f32[32]{0:T(128)}, u32[]{:S(2)}) copy-start(f32[32]{0:T(128)} %copy-done.40) | copy-start | bytes 388
  178.1 48.9 %copy-start.38 = (f32[32]{0:T(128)S(1)}, f32[32]{0:T(128)}, u32[]{:S(2)}) copy-start(f32[32]{0:T(128)} %broadcast_multiply_fusion) | copy-start | bytes 388
  178.1 49.4 %copy-start.34 = (f32[32]{0:T(128)S(1)}, f32[32]{0:T(128)}, u32[]{:S(2)}) copy-start(f32[32]{0:T(128)} %copy-done.33) | copy-start | bytes 388
  178.1 50.1 %copy-start.39 = (f32[32]{0:T(128)S(1)}, f32[32]{0:T(128)}, u32[]{:S(2)}) copy-start(f32[32]{0:T(128)} %get-tuple-element.60) | copy-start | bytes 388
  183.8 51.2 %copy-start.18 = (f32[2048]{0:T(1024)S(1)}, f32[2048]{0:T(1024)}, u32[]{:S(2)}) copy-start(f32[2048]{0:T(1024)} %mul.270) | copy-start | bytes 24580
  190.8 45.0 %copy-start.28 = (f32[32]{0:T(128)}, f32[32]{0:T(128)S(1)}, u32[]{:S(2)}) copy-start(f32[32]{0:T(128)S(1)} %get-tuple-element.50) | copy-start | bytes 388
  235.0 7.4 %copy-start.46 = (f32[32]{0:T(128)}, f32[32]{0:T(128)S(1)}, u32[]{:S(2)}) copy-start(f32[32]{0:T(128)S(1)} %get-tuple-element.114) | copy-start | bytes 388
  253.9 69.0 %copy-start.24 = (f32[32]{0:T(128)S(1)}, f32[32]{0:T(128)}, u32[]{:S(2)}) copy-start(f32[32]{0:T(128)} %copy-done.23) | copy-start | bytes 388
  253.9 69.0 %copy-start.26 = (f32[32]{0:T(128)S(1)}, f32[32]{0:T(128)}, u32[]{:S(2)}) copy-start(f32[32]{0:T(128)} %copy-done.25) | copy-start | bytes 388
  253.9 69.0 %copy-start.32 = (f32[32]{0:T(128)S(1)}, f32[32]{0:T(128)}, u32[]{:S(2)}) copy-start(f32[32]{0:T(128)} %param.21) | copy-start | bytes 388
  253.9 69.0 %copy-start.37 = (f32[32]{0:T(128)S(1)}, f32[32]{0:T(128)}, u32[]{:S(2)}) copy-start(f32[32]{0:T(128)} %param.22) | copy-start | bytes 388
  253.9 81.7 %copy-start.42 = (f32[32]{0:T(128)S(1)}, f32[32]{0:T(128)}, u32[]{:S(2)}) copy-start(f32[32]{0:T(128)} %get-tuple-element.98) | copy-start | bytes 388
  257.3 166.8 %reduce-scatter.5.cloned.1.call-start = ((), (), s32[]{:S(2)}) async-start(), calls=%async_computation.5 | async-start | bytes 2359296 | tf_op jit(solution)/shard_map/reduce_scatter | solution.py:183
  347.6 6.9 %copy-start.13 = (bf16[32,9,256]{2,0,1:T(8,128)(2,1)S(1)}, bf16[32,9,256]{2,0,1:T(8,128)(2,1)}, u32[]{:S(2)}) copy-start(bf16[32,9,256]{2,0,1:T(8,128)(2,1)} %param.20) | copy-start | bytes 442372
  357.9 101.6 %all-reduce.11.cloned.1.call-start = ((), (), s32[]{:S(2)}) async-start(), calls=%async_computation.6 | async-start | bytes 1179648 | tf_op jit(solution)/shard_map/psum | solution.py:187
  365.5 7.4 %copy-start.27 = (f32[32]{0:T(128)S(1)}, f32[32]{0:T(128)}, u32[]{:S(2)}) copy-start(f32[32]{0:T(128)} %copy-done.25) | copy-start | bytes 388
  365.5 7.4 %copy-start.50 = (f32[32]{0:T(128)S(1)}, f32[32]{0:T(128)}, u32[]{:S(2)}) copy-start(f32[32]{0:T(128)} %param.28) | copy-start | bytes 388
  365.5 7.9 %copy-start.29 = (f32[32]{0:T(128)S(1)}, f32[32]{0:T(128)}, u32[]{:S(2)}) copy-start(f32[32]{0:T(128)} %copy-done.28) | copy-start | bytes 388
  365.5 7.9 %copy-start.51 = (f32[32]{0:T(128)S(1)}, f32[32]{0:T(128)}, u32[]{:S(2)}) copy-start(f32[32]{0:T(128)} %param.30) | copy-start | bytes 388
  (9 other events, 18.3 us)
Sparse Core Ops, SparseCore 0:
  10.2 42.8 all-gather.2
  103.9 39.1 all-gather.4
  257.4 65.4 reduce-scatter.2
  358.0 66.0 reduce-scatter.4
  426.9 32.5 all-reduce.10
where the time goes:
time: 472 us; the launch traced here: 471 us
  waiting for transfers between devices  229 us (49%)
  local copies, waits for them, and re-layouts  111 us (24%)
  blocking collectives  64.1 us (14%)
  matrix products  33 us (7%)
  between operations  18.7 us (4%)
  other arithmetic  14.1 us (3%)
    reduce_scatter x1, waiting for transfers between devices, per_device(): lax.psum_scatter(input_piece(conv2_weight, back_second), 'mp', scatter_di...  65.4 us
    reduce_scatter x1, waiting for transfers between devices, per_device(): lax.psum_scatter(input_piece(conv1_weight, back_first), 'mp', scatter_dim...  49.6 us
    all_gather x1, waiting for transfers between devices, per_device(): lax.all_gather(features, 'mp', axis=0, tiled=True)  43 us
    another operation x36, local copies, waits for them, and re-layouts, shifted_taps(): return jnp.stack(pieces)  42.7 us
    unnamed x138, local copies, waits for them, and re-layouts  37.4 us
    all_gather x1, waiting for transfers between devices, per_device(): lax.all_gather(hidden, 'mp', axis=0, tiled=True)  36.8 us
    psum x1, blocking collectives, per_device(): class_logits = lax.psum(partial_logits, 'mp') + head_bias[None, :]  34.9 us
    psum x1, waiting for transfers between devices, per_device(): lax.psum((conv1_grad, conv2_grad, head_grad, head_bias_grad), 'batch')  33.7 us
  transfers between devices with their start and end apart: 5, of which 5 were waited for; matrix products, arithmetic and copies ran while one was open for 4% of the time, Pallas kernels for 0%

commit v1 on v0

--- a/solution.py
+++ b/solution.py
@@ -1,6 +1,10 @@
+import functools
+
 import jax
 import jax.numpy as jnp
 from jax import lax
+from jax.experimental import pallas as pl
+from jax.experimental.pallas import tpu as pltpu
 from jax.sharding import PartitionSpec as P
 
 SIDE = 8
@@ -80,7 +84,7 @@
     return jnp.einsum("otc,ton->cn", weight, back_taps, preferred_element_type=jnp.float32)
 
 
-def per_device(
+def plain_device(
     features,
     counts,
     labels,
@@ -210,9 +214,1050 @@
     )
 
 
+MESH = pl.DeviceIdType.MESH
+F32 = jnp.float32
+BF16 = jnp.bfloat16
+LANES = 128
+PLANE = 2
+
+
+def nn(a, b, precision=None):
+    return lax.dot_general(
+        a, b, (((1,), (0,)), ((), ())), precision=precision, preferred_element_type=F32
+    )
+
+
+def nt(a, b, precision=None):
+    return lax.dot_general(
+        a, b, (((1,), (1,)), ((), ())), precision=precision, preferred_element_type=F32
+    )
+
+
+def tn(a, b, precision=None):
+    return lax.dot_general(
+        a, b, (((0,), (0,)), ((), ())), precision=precision, preferred_element_type=F32
+    )
+
+
+def rows_first(field, images):
+    return jnp.concatenate(
+        [
+            field[(m * SIDE + i) * SIDE : (m * SIDE + i + 1) * SIDE]
+            for i in range(SIDE)
+            for m in range(images)
+        ]
+    )
+
+
+def images_first(field, images):
+    return jnp.concatenate(
+        [
+            field[(i * images + m) * SIDE : (i * images + m + 1) * SIDE]
+            for m in range(images)
+            for i in range(SIDE)
+        ]
+    )
+
+
+def store_taps(put, field, block):
+    cells, width = field.shape
+    tiles = field.reshape(cells // SIDE, SIDE, width)
+    column = lax.broadcasted_iota(jnp.int32, tiles.shape, 1)
+    left = jnp.where(column == 0, 0.0, pltpu.roll(tiles, 1, 1)).reshape(cells, width)
+    right = jnp.where(column == SIDE - 1, 0.0, pltpu.roll(tiles, SIDE - 1, 1)).reshape(
+        cells, width
+    )
+    for lateral, shifted in enumerate((left, field, right)):
+        put(lateral, pl.ds(block, cells), shifted.astype(BF16))
+
+
+def row_sum(field):
+    return jnp.sum(field, axis=0, keepdims=True)
+
+
+def halves(row):
+    return [row[:, at : at + LANES] for at in range(0, row.shape[1], LANES)]
+
+
+def image_terms(logits, teacher, labels):
+    def parts(values):
+        top = jnp.max(values, axis=1, keepdims=True)
+        weights = jnp.exp(values - top)
+        total = jnp.sum(weights, axis=1, keepdims=True)
+        return top + jnp.log(total), weights / total
+
+    onehot = (
+        labels == lax.broadcasted_iota(jnp.int32, logits.shape, 1)
+    ).astype(F32)
+    full_lse, full_soft = parts(logits)
+    pupil = logits / softening_heat
+    mentor = teacher / softening_heat
+    pupil_rest = pupil - 1000.0 * onehot
+    mentor_rest = mentor - 1000.0 * onehot
+    pupil_all, pupil_soft = parts(pupil)
+    mentor_all, _ = parts(mentor)
+    pupil_other, pupil_rest_soft = parts(pupil_rest)
+    mentor_other, mentor_rest_soft = parts(mentor_rest)
+
+    def pick(values):
+        return jnp.sum(onehot * values, axis=1, keepdims=True)
+
+    pupil_hit = pick(pupil) - pupil_all
+    mentor_hit = pick(mentor) - mentor_all
+    pupil_miss = pupil_other - pupil_all
+    mentor_miss = mentor_other - mentor_all
+    hit_weight, miss_weight = jnp.exp(mentor_hit), jnp.exp(mentor_miss)
+    binary = hit_weight * (mentor_hit - pupil_hit) + miss_weight * (
+        mentor_miss - pupil_miss
+    )
+    gap = (mentor_rest - mentor_other) - (pupil_rest - pupil_other)
+    spread = jnp.sum(mentor_rest_soft * gap, axis=1, keepdims=True)
+    squared = softening_heat * softening_heat
+    value = (
+        full_lse
+        - pick(logits)
+        + squared * (target_weight * binary + other_weight * spread)
+    )
+    binary_slope = (
+        (hit_weight + miss_weight) * pupil_soft
+        - hit_weight * onehot
+        - miss_weight * pupil_rest_soft
+    )
+    spread_slope = pupil_rest_soft - mentor_rest_soft
+    slope = (
+        full_soft
+        - onehot
+        + softening_heat
+        * (target_weight * binary_slope + other_weight * spread_slope)
+    )
+    return value, slope
+
+
+def block_kernel(
+    sizes,
+    features,
+    counts,
+    labels,
+    teacher,
+    conv1,
+    conv2,
+    head_weight,
+    head_bias,
+    *rest,
+):
+    params, rest = rest[:8], rest[8:]
+    (
+        out_features,
+        out_conv1,
+        out_conv2,
+        out_small,
+        weight1,
+        weight2,
+        teacher_here,
+        labels_here,
+        head_here,
+        head_bias_here,
+        params_here,
+        cells_in,
+        params_all,
+        counts_all,
+        head_all,
+        sums_all,
+        logit_stage,
+        logit_all,
+        field,
+        normed1,
+        slope1,
+        normed2,
+        grad_pre2,
+        taps_x,
+        taps_h,
+        taps_g,
+        raw_x,
+        raw_h,
+        layer_x,
+        layer_h,
+        grad_stage,
+        grad_all,
+        column_part,
+        column_stage,
+        column_all,
+        mean_all,
+        edge_part,
+        edge_all,
+        quarter_all,
+        cells_stage,
+        cells_out,
+        load_sem,
+        send_sem,
+        sums_send,
+        sums_recv,
+        logit_send,
+        logit_recv,
+        cells_recv,
+        params_recv,
+        counts_recv,
+        head_recv,
+        weight_recv,
+        raw_recv,
+        grad_recv,
+        column_recv,
+        mean_recv,
+        edge_recv,
+        quarter_recv,
+        out_recv,
+    ) = rest
+    n_batch, n_mp, channels, images = sizes
+    n_z = n_mp // PLANE
+    width = channels // n_mp
+    quarter = width // n_batch
+    block = images * SIDE
+    cells = block * SIDE
+    everyone = n_batch * n_mp
+    b, p = lax.axis_index("batch"), lax.axis_index("mp")
+    x, c = b // PLANE, b % PLANE
+    z, y = p // PLANE, p % PLANE
+    me = b * n_mp + p
+    seat = y * n_batch + b
+    tall = column_part.shape[2]
+    means_end_value = {}
+    sent = []
+
+    def send(src, dst, recv, to_b, to_p):
+        copy = pltpu.make_async_remote_copy(
+            src_ref=src,
+            dst_ref=dst,
+            send_sem=send_sem.at[len(sent)],
+            recv_sem=recv,
+            device_id=(to_b, to_p),
+            device_id_type=MESH,
+        )
+        copy.start()
+        sent.append(copy)
+
+    def await_bytes(ref, sem):
+        pltpu.make_async_copy(ref, ref, sem).wait()
+
+    others = [
+        ((b + j) % n_batch, (p + k) % n_mp)
+        for k in range(n_mp)
+        for j in range(n_batch)
+        if j or k
+    ]
+
+    loads = [
+        (conv1, weight1.at[:, pl.ds(pl.multiple_of(p * width, width), width), :]),
+        (conv2, weight2.at[:, pl.ds(pl.multiple_of(p * width, width), width), :]),
+        (teacher, teacher_here),
+        (labels, labels_here),
+        (head_weight, head_here),
+        (head_bias, head_bias_here),
+    ] + [(ref, params_here.at[i]) for i, ref in enumerate(params)]
+    loads = [
+        pltpu.make_async_copy(src, dst, load_sem.at[i])
+        for i, (src, dst) in enumerate(loads)
+    ]
+    for load in loads:
+        load.start()
+    barrier = pltpu.get_barrier_semaphore()
+    for to_b, to_p in others:
+        pl.semaphore_signal(
+            barrier, inc=1, device_id=(to_b, to_p), device_id_type=MESH
+        )
+
+    for taps in (taps_x, taps_h, taps_g):
+        for lateral in range(3):
+            taps[lateral, 0:block] = jnp.zeros((block, channels), BF16)
+            taps[lateral, block + cells : 2 * block + cells] = jnp.zeros(
+                (block, channels), BF16
+            )
+    for layer in (layer_x, layer_h):
+        for s in range(n_batch * PLANE):
+            for lateral in range(3):
+                layer[s, lateral, 0:block] = jnp.zeros((block, channels), BF16)
+                layer[s, lateral, block + cells : 2 * block + cells] = jnp.zeros(
+                    (block, channels), BF16
+                )
+    for load in loads:
+        load.wait()
+    group = LANES // width
+    place = pl.multiple_of((p % group) * width, width)
+    own_params = jnp.concatenate(
+        [params_here[i] for i in range(4)] + [jnp.zeros((4, width), F32)]
+    )
+    own_params = jnp.concatenate(
+        [own_params, jnp.zeros((8, LANES - width), F32)], axis=1
+    )
+    params_all[p] = pltpu.roll(own_params, place, 1)
+    count = counts[0]
+    counts_all[b] = jnp.zeros((8, LANES), F32) + count.astype(F32)
+    head_all[p] = head_here[...]
+
+    pl.semaphore_wait(barrier, everyone - 1)
+
+    half = pl.ds(pl.multiple_of(c * LANES, LANES), LANES)
+    strip = width // PLANE
+
+    def rows_of(at_z, at_y, at_x):
+        start = (at_z * PLANE + at_y) * width + at_x * strip
+        return pl.ds(pl.multiple_of(start, strip), strip)
+
+    far = [lambda v: n_z - 1 - v, lambda v: (v + n_z // 2) % n_z]
+    if n_z == 4:
+        far.append(lambda v: v + 1 - 2 * (v % 2))
+    mates = [(1, 1), (1, 0), (0, 1)]
+
+    def column_start(which, weight):
+        part = weight.at[:, rows_of(z, y, x), half]
+        for k, other in enumerate(far):
+            send(part, part, weight_recv.at[which, k], b, other(z) * PLANE + y)
+
+    def shard_start(which, weight):
+        part = weight.at[
+            :, pl.ds(pl.multiple_of(p * width, width), width), half
+        ]
+        send(part, part, weight_recv.at[which, 3], b, z * PLANE + 1 - y)
+
+    def layer_start(which, weight):
+        for k, other in enumerate(far):
+            part = weight.at[:, rows_of(other(z), y, x), half]
+            await_bytes(part, weight_recv.at[which, k])
+            for i, (dx, dy) in enumerate(mates):
+                send(
+                    part,
+                    part,
+                    weight_recv.at[which, 4 + 3 * k + i],
+                    ((x + dx) % 2) * PLANE + c,
+                    z * PLANE + (y + dy) % 2,
+                )
+
+    def core_start(which, weight):
+        part = weight.at[
+            :,
+            pl.ds(
+                pl.multiple_of((z * PLANE + 1 - y) * width, width), width
+            ),
+            half,
+        ]
+        await_bytes(part, weight_recv.at[which, 3])
+        send(part, part, weight_recv.at[which, 13], x * PLANE + 1 - c, p)
+        for k, other in enumerate(far):
+            for i, (dx, dy) in enumerate(mates):
+                part = weight.at[
+                    :, rows_of(other(z), (y + dy) % 2, (x + dx) % 2), half
+                ]
+                await_bytes(part, weight_recv.at[which, 4 + 3 * k + i])
+            part = weight.at[
+                :,
+                pl.ds(
+                    pl.multiple_of(other(z) * PLANE * width, PLANE * width),
+                    PLANE * width,
+                ),
+                half,
+            ]
+            send(part, part, weight_recv.at[which, 14 + k], x * PLANE + 1 - c, p)
+
+    def core_end(which, weight):
+        theirs = pl.ds(pl.multiple_of((1 - c) * LANES, LANES), LANES)
+        part = weight.at[
+            :,
+            pl.ds(
+                pl.multiple_of((z * PLANE + 1 - y) * width, width), width
+            ),
+            theirs,
+        ]
+        await_bytes(part, weight_recv.at[which, 13])
+        for k, other in enumerate(far):
+            part = weight.at[
+                :,
+                pl.ds(
+                    pl.multiple_of(other(z) * PLANE * width, PLANE * width),
+                    PLANE * width,
+                ),
+                theirs,
+            ]
+            await_bytes(part, weight_recv.at[which, 14 + k])
+
+    column_start(0, weight1)
+    shard_start(0, weight1)
+
+    def cells_of(q):
+        return pl.ds(pl.multiple_of(q * cells, cells), cells)
+
+    own_cells = pltpu.make_async_copy(
+        features.at[:, cells_of(p)], cells_in.at[p], load_sem.at[0]
+    )
+    own_cells.start()
+    for k in range(1, n_mp):
+        q = (p + k) % n_mp
+        send(features.at[:, cells_of(q)], cells_in.at[p], cells_recv.at[k], b, q)
+    for k in range(1, n_mp):
+        q = (p + k) % n_mp
+        send(params_all.at[p], params_all.at[p], params_recv.at[k], b, q)
+        send(head_all.at[p], head_all.at[p], head_recv.at[k], b, q)
+    for j in range(1, n_batch):
+        send(
+            counts_all.at[b],
+            counts_all.at[b],
+            counts_recv.at[j],
+            (b + j) % n_batch,
+            p,
+        )
+
+    layer_start(0, weight1)
+    column_start(1, weight2)
+    own_cells.wait()
+    for k in range(1, n_mp):
+        q = (p + n_mp - k) % n_mp
+        await_bytes(cells_in.at[q], cells_recv.at[k])
+    by_channel = cells_in[...].reshape(channels, cells).astype(F32)
+    by_cell = rows_first(by_channel.T, images)
+    field[...] = by_cell
+
+    def put_x(lateral, where, value):
+        taps_x[lateral, where] = value
+
+    store_taps(put_x, by_cell, block)
+    raw_x[seat] = by_cell.astype(BF16)
+
+    core_start(0, weight1)
+
+    for k in range(1, n_mp):
+        q = (p + n_mp - k) % n_mp
+        await_bytes(params_all.at[q], params_recv.at[k])
+        await_bytes(head_all.at[q], head_recv.at[k])
+    for j in range(1, n_batch):
+        await_bytes(counts_all.at[(b + n_batch - j) % n_batch], counts_recv.at[j])
+    full_params = jnp.concatenate(
+        [
+            sum(params_all[q] for q in range(at, at + group))
+            for at in range(0, n_mp, group)
+        ],
+        axis=1,
+    )
+    gain1, bias1, gain2, bias2 = (full_params[i : i + 1] for i in range(4))
+    live_images = sum(counts_all[i] for i in range(n_batch))[0:1, 0:1]
+    live_cells = live_images * float(SIDE * SIDE)
+
+    slot = (lax.broadcasted_iota(jnp.int32, (cells, channels), 0) // SIDE) % images
+    live = (slot + p * images < count).astype(F32)
+
+    shape = (cells, LANES)
+    cell = lax.broadcasted_iota(jnp.int32, shape, 0)
+    tap_at = lax.broadcasted_iota(jnp.int32, shape, 1)
+    down = (tap_at >= 3).astype(jnp.int32) + (tap_at >= 6).astype(jnp.int32)
+    across = tap_at - 3 * down
+    at_row = cell // block + down - 1
+    at_column = cell % SIDE + across - 1
+    within = (at_row >= 0) & (at_row < SIDE) & (at_column >= 0) & (at_column < SIDE)
+    inside = jnp.where(within & (tap_at < 9), 1.0, 0.0).astype(BF16)
+
+    def conv(taps, weight):
+        total = None
+        for tap in range(9):
+            vertical, lateral = divmod(tap, 3)
+            term = nt(
+                taps[lateral, block * vertical : block * vertical + cells],
+                weight[tap],
+            )
+            total = term if total is None else total + term
+        return total
+
+    def conv_back(taps, weight):
+        total = None
+        for tap in range(9):
+            vertical, lateral = divmod(tap, 3)
+            up = block * (2 - vertical)
+            term = nn(taps[2 - lateral, up : up + cells], weight[tap])
+            total = term if total is None else total + term
+        return total
+
+    def sums_start(which, one, two):
+        mine = sums_all.at[which, me, pl.ds(0, 4)]
+        sums_all[which, me, 0:4] = jnp.concatenate(halves(one) + halves(two))
+        for to_b, to_p in reversed(others):
+            pltpu.make_async_remote_copy(
+                src_ref=mine,
+                dst_ref=mine,
+                send_sem=sums_send.at[which],
+                recv_sem=sums_recv.at[which],
+                device_id=(to_b, to_p),
+                device_id_type=MESH,
+            ).start()
+
+    def sums_end(which):
+        everything = sums_all.at[which, pl.ds(0, everyone - 1), pl.ds(0, 4)]
+        await_bytes(everything, sums_recv.at[which])
+        total = jnp.sum(sums_all[which], axis=0)
+        return (
+            jnp.concatenate([total[0:1], total[1:2]], axis=1),
+            jnp.concatenate([total[2:3], total[3:4]], axis=1),
+        )
+
+    def means_start(which, value):
+        mean_all[which, z] = jnp.concatenate(
+            halves(row_sum(value) / float(cells))
+            + [jnp.zeros((8 - channels // LANES, LANES), F32)]
+        )
+        part = mean_all.at[which, z]
+        for k, other in enumerate(far):
+            send(part, part, mean_recv.at[which, k], b, other(z) * PLANE + y)
+
+    def means_end(which):
+        for k, other in enumerate(far):
+            await_bytes(mean_all.at[which, other(z)], mean_recv.at[which, k])
+        total = sum(mean_all[which, at_z] for at_z in range(n_z)) / float(n_z)
+        return jnp.concatenate(
+            [total[i : i + 1] for i in range(channels // LANES)], axis=1
+        )
+
+    def raw_start(which, raw):
+        part = raw.at[seat]
+        for i, (dx, dy) in enumerate(mates):
+            send(
+                part,
+                part,
+                raw_recv.at[which, i],
+                ((x + dx) % 2) * PLANE + c,
+                z * PLANE + (y + dy) % 2,
+            )
+        send(part, part, raw_recv.at[which, 3], x * PLANE + 1 - c, p)
+
+    def seat_of(dx, dy, dc):
+        return ((y + dy) % 2) * n_batch + ((x + dx) % 2) * PLANE + (c + dc) % 2
+
+    def raw_forward(which, raw):
+        for i, (dx, dy) in enumerate(mates):
+            part = raw.at[seat_of(dx, dy, 0)]
+            await_bytes(part, raw_recv.at[which, i])
+            send(part, part, raw_recv.at[which, 4 + i], x * PLANE + 1 - c, p)
+
+    def raw_end(which, raw, layer):
+        await_bytes(raw.at[seat_of(0, 0, 1)], raw_recv.at[which, 3])
+        for i, (dx, dy) in enumerate(mates):
+            await_bytes(raw.at[seat_of(dx, dy, 1)], raw_recv.at[which, 4 + i])
+
+        def build(s, carry):
+            def put(lateral, where, value):
+                layer[s, lateral, where] = value
+
+            store_taps(put, raw[s].astype(F32), block)
+            return carry
+
+        lax.fori_loop(0, n_batch * PLANE, build, 0)
+
+    seats = [
+        (dx, dy, dc)
+        for dy in (1, 0)
+        for dx in (1, 0)
+        for dc in (1, 0)
+        if dx or dy or dc
+    ]
+
+    def grads_start(which, grad):
+        by_row = grad.T
+        for s in range(n_batch * PLANE):
+            at_y, at_b = divmod(s, n_batch)
+            grad_stage[which, s] = jnp.concatenate(
+                [
+                    by_row[start : start + quarter]
+                    for start in (
+                        (at_z * PLANE + at_y) * width + at_b * quarter
+                        for at_z in range(n_z)
+                    )
+                ]
+            ).astype(BF16)
+        for i, (dx, dy, dc) in enumerate(seats):
+            send(
+                grad_stage.at[which, seat_of(dx, dy, dc)],
+                grad_all.at[which, seat],
+                grad_recv.at[which, i],
+                ((x + dx) % 2) * PLANE + (c + dc) % 2,
+                z * PLANE + (y + dy) % 2,
+            )
+        grad_all[which, seat] = grad_stage[which, seat]
+
+    def grads_end(which, layer):
+        for i, (dx, dy, dc) in enumerate(seats):
+            await_bytes(grad_all.at[which, seat_of(dx, dy, dc)], grad_recv.at[which, i])
+        mean = means_end(1 - which)
+        means_end_value[which] = mean
+        edges = sum(nn(grad_all[which, s], inside) for s in range(n_batch * PLANE))
+        for at_z in range(n_z):
+            edge_part[which, at_z] = edges[at_z * quarter : (at_z + 1) * quarter]
+        for tap in range(9):
+            vertical, lateral = divmod(tap, 3)
+            total = -edges[:, tap : tap + 1] * mean
+            for s in range(n_batch * PLANE):
+                term = nn(
+                    grad_all[which, s],
+                    layer[s, lateral, block * vertical : block * vertical + cells],
+                )
+                total = total + term
+            for at_z in range(n_z):
+                column_part[which, at_z, tap * quarter : (tap + 1) * quarter] = total[
+                    at_z * quarter : (at_z + 1) * quarter
+                ]
+        for at_z in range(n_z):
+            column_stage[which, at_z] = column_part[which, at_z].astype(BF16)
+        for k, other in enumerate(far):
+            send(
+                column_stage.at[which, other(z)],
+                column_all.at[which, k],
+                column_recv.at[which, k],
+                b,
+                other(z) * PLANE + y,
+            )
+            send(
+                edge_part.at[which, other(z)],
+                edge_all.at[which, k],
+                edge_recv.at[which, k],
+                b,
+                other(z) * PLANE + y,
+            )
+
+    def quarters_start(which):
+        for k in range(len(far)):
+            await_bytes(column_all.at[which, k], column_recv.at[which, k])
+            await_bytes(edge_all.at[which, k], edge_recv.at[which, k])
+        mean = means_end_value[which]
+        edges = edge_part[which, z]
+        total = column_part[which, z]
+        for k in range(len(far)):
+            edges = edges + edge_all[which, k]
+            total = total + column_all[which, k].astype(F32)
+        back = jnp.concatenate(
+            [edges[:, tap : tap + 1] * mean for tap in range(9)]
+            + [jnp.zeros((tall - 9 * quarter, channels), F32)]
+        )
+        quarter_all[which, b] = (total + back).astype(BF16)
+        for j in range(1, n_batch):
+            part = quarter_all.at[which, b]
+            send(part, part, quarter_recv.at[which, j], (b + j) % n_batch, p)
+
+    def quarters_end(which, out):
+        for j in range(1, n_batch):
+            await_bytes(
+                quarter_all.at[which, (b + n_batch - j) % n_batch],
+                quarter_recv.at[which, j],
+            )
+        for at_b in range(n_batch):
+            whole = quarter_all[which, at_b].astype(F32)
+            for tap in range(9):
+                out[tap, at_b * quarter : (at_b + 1) * quarter] = whole[
+                    tap * quarter : (tap + 1) * quarter
+                ]
+
+    for which in range(2):
+        for at_z in range(n_z):
+            column_part[which, at_z, 9 * quarter :] = jnp.zeros(
+                (tall - 9 * quarter, channels), F32
+            )
+
+    means_start(0, by_cell)
+    core_end(0, weight1)
+    first = conv(taps_x, weight1)
+    masked = first * live
+    sums_start(0, row_sum(masked), row_sum(masked * first))
+    shard_start(1, weight2)
+    layer_start(1, weight2)
+    total, square = sums_end(0)
+    mean1 = total / live_cells
+    var1 = square / live_cells - mean1 * mean1
+    rstd1 = lax.rsqrt(var1 + epsilon)
+    flat = (first - mean1) * rstd1
+    normed1[...] = flat
+    pre1 = gain1 * flat + bias1
+    sigma1 = jax.nn.sigmoid(pre1)
+    slope1[...] = sigma1 * (1.0 + pre1 * (1.0 - sigma1))
+    hidden = pre1 * sigma1
+
+    def put_h(lateral, where, value):
+        taps_h[lateral, where] = value
+
+    store_taps(put_h, hidden, block)
+    raw_h[seat] = hidden.astype(BF16)
+    means_start(1, hidden)
+    core_start(1, weight2)
+    core_end(1, weight2)
+
+    second = conv(taps_h, weight2)
+    masked = second * live
+    sums_start(1, row_sum(masked), row_sum(masked * second))
+    raw_start(1, raw_h)
+    total, square = sums_end(1)
+    mean2 = total / live_cells
+    var2 = square / live_cells - mean2 * mean2
+    rstd2 = lax.rsqrt(var2 + epsilon)
+    flat2 = (second - mean2) * rstd2
+    normed2[...] = flat2
+    pre2 = gain2 * flat2 + bias2 + field[...]
+    sigma2 = jax.nn.sigmoid(pre2)
+    block_out = pre2 * sigma2
+
+    pooled = sum(block_out[i * block : (i + 1) * block] for i in range(SIDE))
+    pooled = jnp.sum(pooled.reshape(images, SIDE, channels), axis=1) / float(
+        SIDE * SIDE
+    )
+    head = head_all[...].reshape(channels, head_all.shape[2]).astype(F32)
+    logits = nn(pooled, head, highest) + head_bias_here[...]
+    slots = labels_here.shape[1]
+    image_at = lax.broadcasted_iota(jnp.int32, (images, slots), 0) + p * images
+    picked = lax.broadcasted_iota(jnp.int32, (images, slots), 1) == image_at
+    own_labels = jnp.sum(
+        jnp.where(picked, labels_here[...], 0), axis=1, keepdims=True
+    )
+    own_teacher = nn(picked.astype(F32), teacher_here[...], highest)
+    own_live = (image_at[:, 0:1] < count).astype(F32)
+    per_image, slope = image_terms(logits, own_teacher, own_labels)
+    grad_logits = slope * (own_live * (loss_scale / live_images))
+    grad_pooled = nt(grad_logits, head, highest) / float(SIDE * SIDE)
+    spread = jnp.concatenate(
+        [
+            jnp.broadcast_to(grad_pooled[m : m + 1], (SIDE, channels))
+            for m in range(images)
+        ]
+    )
+    spread = jnp.concatenate([spread] * SIDE)
+    pre_grad2 = spread * (sigma2 * (1.0 + pre2 * (1.0 - sigma2)))
+    grad_pre2[...] = pre_grad2
+    sums_start(2, row_sum(pre_grad2), row_sum(pre_grad2 * flat2))
+
+    raw_start(0, raw_x)
+    raw_forward(1, raw_h)
+    raw_end(1, raw_h, layer_h)
+
+    bias_grad2, gain_grad2 = sums_end(2)
+    grad_second = (gain2 * rstd2) * (
+        grad_pre2[...]
+        - live * (bias_grad2 + normed2[...] * gain_grad2) / live_cells
+    )
+    grads_start(0, grad_second)
+
+    def put_g(lateral, where, value):
+        taps_g[lateral, where] = value
+
+    store_taps(put_g, grad_second.astype(BF16).astype(F32), block)
+    pre_grad1 = conv_back(taps_g, weight2) * slope1[...]
+    sums_start(3, row_sum(pre_grad1), row_sum(pre_grad1 * normed1[...]))
+    classes = logits.shape[1]
+    for q in range(n_mp):
+        logit_stage[q] = jnp.zeros((2 * images, LANES), F32)
+        logit_stage[q, 0:images, 0:classes] = grad_logits
+        logit_stage[q, 0:images, classes : classes + 1] = own_live * per_image
+        logit_stage[q, images : 2 * images, 0:width] = pooled[
+            :, q * width : (q + 1) * width
+        ]
+    for to_b, to_p in others:
+        pltpu.make_async_remote_copy(
+            src_ref=logit_stage.at[to_p],
+            dst_ref=logit_all.at[me],
+            send_sem=logit_send,
+            recv_sem=logit_recv,
+            device_id=(to_b, to_p),
+            device_id_type=MESH,
+        ).start()
+    logit_all[me] = logit_stage[p]
+    grads_end(0, layer_h)
+    raw_forward(0, raw_x)
+    raw_end(0, raw_x, layer_x)
+    bias_grad1, gain_grad1 = sums_end(3)
+    grad_first = (gain1 * rstd1) * (
+        pre_grad1 - live * (bias_grad1 + normed1[...] * gain_grad1) / live_cells
+    )
+    grads_start(1, grad_first)
+    store_taps(put_g, grad_first.astype(BF16).astype(F32), block)
+    grad_in = conv_back(taps_g, weight1) + grad_pre2[...]
+    cells_stage[...] = (
+        images_first(grad_in, images).T.astype(BF16).reshape(n_mp, width, cells)
+    )
+    for k in range(1, n_mp):
+        q = (p + k) % n_mp
+        send(cells_stage.at[q], cells_out.at[p], out_recv.at[k], b, q)
+    cells_out[p] = cells_stage[p]
+    grads_end(1, layer_x)
+    quarters_start(0)
+    quarters_start(1)
+
+    def own(row):
+        pieces = halves(row)
+        mine = pieces[0]
+        for i in range(1, len(pieces)):
+            mine = jnp.where(p // group == i, pieces[i], mine)
+        return pltpu.roll(mine, (LANES - place) % LANES, 1)[:, 0:width]
+
+    adjust = live_cells / (live_cells - 1.0)
+    kept = 1.0 - momentum
+    rows = [
+        own(gain_grad1),
+        own(bias_grad1),
+        own(gain_grad2),
+        own(bias_grad2),
+        kept * params_here[4] + momentum * own(mean1),
+        kept * params_here[5] + momentum * own(var1 * adjust),
+        kept * params_here[6] + momentum * own(mean2),
+        kept * params_here[7] + momentum * own(var2 * adjust),
+    ]
+    out_small[...] = jnp.zeros_like(out_small)
+    for i, row in enumerate(rows):
+        out_small[i : i + 1, 0:width] = row
+    await_bytes(logit_all.at[pl.ds(0, everyone - 1)], logit_recv)
+    tall = logit_all[...]
+    upper = lax.broadcasted_iota(jnp.int32, tall.shape, 1) < images
+    upper_logits = jnp.where(upper, tall, 0.0).reshape(-1, LANES)
+    lifted = jnp.where(upper, pltpu.roll(tall, images, 1), 0.0).reshape(-1, LANES)
+    out_small[16 : 16 + width] = tn(lifted, upper_logits, highest)[0:width]
+    columns = row_sum(upper_logits)
+    out_small[8:9] = columns
+    out_small[9:10] = jnp.broadcast_to(
+        columns[:, classes : classes + 1] / live_images, (1, LANES)
+    )
+
+    quarters_end(0, out_conv2)
+    for k in range(1, n_mp):
+        q = (p + n_mp - k) % n_mp
+        await_bytes(cells_out.at[q], out_recv.at[k])
+    for q in range(n_mp):
+        out_features[:, q * cells : (q + 1) * cells] = cells_out[q].astype(F32)
+    quarters_end(1, out_conv1)
+
+    for copy in sent:
+        copy.wait_send()
+    for which in range(4):
+        await_bytes(
+            sums_all.at[which, pl.ds(0, everyone - 1), pl.ds(0, 4)],
+            sums_send.at[which],
+        )
+    await_bytes(logit_all.at[pl.ds(0, everyone - 1)], logit_send)
+
+
+def finish_kernel(
+    features_in,
+    conv1_in,
+    conv2_in,
+    small,
+    loss,
+    features_out,
+    conv1_out,
+    gain1_out,
+    bias1_out,
+    conv2_out,
+    gain2_out,
+    bias2_out,
+    head_out,
+    head_bias_out,
+    *stats_out,
+):
+    features_out[...] = features_in[...]
+    conv1_out[...] = conv1_in[...]
+    conv2_out[...] = conv2_in[...]
+    vectors = (gain1_out, bias1_out, gain2_out, bias2_out) + stats_out
+    for i, out in enumerate(vectors):
+        out[...] = small[i : i + 1, 0 : out.shape[1]]
+    head_bias_out[...] = small[8:9, 0 : head_bias_out.shape[1]]
+    loss[0] = small[9, 0]
+    head_out[...] = small[16 : 16 + head_out.shape[0], 0 : head_out.shape[1]]
+
+
+def block_device(
+    n_batch,
+    n_mp,
+    features,
+    counts,
+    labels,
+    teacher,
+    conv1_weight,
+    bn1_gain,
+    bn1_bias,
+    conv2_weight,
+    bn2_gain,
+    bn2_bias,
+    head_weight,
+    head_bias,
+    run_mean1,
+    run_var1,
+    run_mean2,
+    run_var2,
+):
+    width, cell_count = features.shape
+    channels = width * n_mp
+    classes = head_weight.shape[1]
+    slots = cell_count // (SIDE * SIDE)
+    images = slots // n_mp
+    block = images * SIDE
+    cells = block * SIDE
+    n_z = n_mp // PLANE
+    quarter = width // n_batch
+    seats = n_batch * PLANE
+    everyone = n_batch * n_mp
+    tall = -(-9 * quarter // 16) * 16
+    padded = cells + 2 * block
+
+    def row(values):
+        return values.reshape(1, -1)
+
+    def taps_out(values):
+        return values.transpose(1, 0, 2)
+
+    def vmem(*shape, dtype=F32):
+        return pltpu.VMEM(shape, dtype)
+
+    def low(*shape):
+        return pltpu.VMEM(shape, BF16)
+
+    any_space = pl.BlockSpec(memory_space=pl.ANY)
+    in_vmem = pl.BlockSpec(memory_space=pltpu.VMEM)
+    in_smem = pl.BlockSpec(memory_space=pltpu.SMEM)
+    shape = jax.ShapeDtypeStruct
+    dma = pltpu.SemaphoreType.DMA
+    grant = pltpu.CompilerParams(
+        collective_id=0, has_side_effects=True, vmem_limit_bytes=60 * 2**20
+    )
+    packed = pl.pallas_call(
+        functools.partial(block_kernel, (n_batch, n_mp, channels, images)),
+        out_shape=(
+            shape((width, cell_count), F32),
+            shape((9, width, channels), F32),
+            shape((9, width, channels), F32),
+            shape((16 + width, LANES), F32),
+        ),
+        in_specs=[any_space, in_smem] + [any_space] * 14,
+        out_specs=(in_vmem,) * 4,
+        scratch_shapes=[
+            low(9, channels, channels),
+            low(9, channels, channels),
+            vmem(slots, classes),
+            vmem(1, slots, dtype=jnp.int32),
+            low(width, classes),
+            vmem(1, classes),
+            vmem(8, 1, width),
+            low(n_mp, width, cells),
+            vmem(n_mp, 8, LANES),
+            vmem(n_batch, 8, LANES),
+            low(n_mp, width, classes),
+            vmem(4, everyone, 8, LANES),
+            vmem(n_mp, 2 * images, LANES),
+            vmem(everyone, 2 * images, LANES),
+            vmem(cells, channels),
+            vmem(cells, channels),
+            vmem(cells, channels),
+            vmem(cells, channels),
+            vmem(cells, channels),
+            low(3, padded, channels),
+            low(3, padded, channels),
+            low(3, padded, channels),
+            low(seats, cells, channels),
+            low(seats, cells, channels),
+            low(seats, 3, padded, channels),
+            low(seats, 3, padded, channels),
+            low(2, seats, n_z * quarter, cells),
+            low(2, seats, n_z * quarter, cells),
+            vmem(2, n_z, tall, channels),
+            low(2, n_z, tall, channels),
+            low(2, n_z - 1, tall, channels),
+            vmem(2, n_z, 8, LANES),
+            vmem(2, n_z, quarter, LANES),
+            vmem(2, n_z - 1, quarter, LANES),
+            low(2, n_batch, tall, channels),
+            low(n_mp, width, cells),
+            low(n_mp, width, cells),
+            dma((14,)),
+            dma((128,)),
+            dma((4,)),
+            dma((4,)),
+            dma,
+            dma,
+            dma((n_mp,)),
+            dma((n_mp,)),
+            dma((n_batch,)),
+            dma((n_mp,)),
+            dma((2, 17)),
+            dma((2, 7)),
+            dma((2, 7)),
+            dma((2, n_z - 1)),
+            dma((2, n_z - 1)),
+            dma((2, n_z - 1)),
+            dma((2, n_batch)),
+            dma((n_mp,)),
+        ],
+        compiler_params=grant,
+    )(
+        features,
+        counts,
+        row(labels),
+        teacher,
+        taps_out(conv1_weight),
+        taps_out(conv2_weight),
+        head_weight,
+        row(head_bias),
+        row(bn1_gain),
+        row(bn1_bias),
+        row(bn2_gain),
+        row(bn2_bias),
+        row(run_mean1),
+        row(run_var1),
+        row(run_mean2),
+        row(run_var2),
+    )
+    vector = shape((1, width), F32)
+    results = pl.pallas_call(
+        finish_kernel,
+        out_shape=(
+            shape((1,), F32),
+            shape((width, cell_count), F32),
+            shape((9, width, channels), F32),
+            vector,
+            vector,
+            shape((9, width, channels), F32),
+            vector,
+            vector,
+            shape((width, classes), F32),
+            shape((1, classes), F32),
+            vector,
+            vector,
+            vector,
+            vector,
+        ),
+        in_specs=[in_vmem] * 4,
+        out_specs=(in_smem,) + (in_vmem,) * 13,
+        compiler_params=pltpu.CompilerParams(vmem_limit_bytes=60 * 2**20),
+    )(*packed)
+    loss, grad_features, conv1, gain1, bias1, conv2, gain2, bias2, head, *small = results
+    return (
+        loss.reshape(()),
+        grad_features,
+        taps_out(conv1),
+        gain1.reshape(-1),
+        bias1.reshape(-1),
+        taps_out(conv2),
+        gain2.reshape(-1),
+        bias2.reshape(-1),
+        head,
+    ) + tuple(values.reshape(-1) for values in small)
+
+
+def by_images(n_batch, n_mp, features, counts, *rest):
+    width, cell_count = features.shape
+    images = cell_count // (SIDE * SIDE) // n_mp
+    fits = (
+        n_batch == 4
+        and n_mp == 8
+        and width == 32
+        and images == 4
+        and head_fits(rest)
+    )
+    if not fits:
+        return plain_device(features, counts, *rest)
+    return block_device(n_batch, n_mp, features, counts, *rest)
+
+
+def head_fits(rest):
+    return rest[8].shape[1] < LANES
+
+
 def solution(mesh):
     return jax.shard_map(
-        per_device,
+        functools.partial(by_images, mesh.shape["batch"], mesh.shape["mp"]),
         mesh=mesh,
         in_specs=(
             P("mp", "batch"),

time: 472 us -> 73.8 us (0.16)
  waiting for transfers between devices: 229 us -> 0 us
  local copies, waits for them, and re-layouts: 111 us -> 0 us
  Pallas kernels: 0 us -> 72.3 us
  blocking collectives: 64.1 us -> 0 us
  matrix products: 33 us -> 0 us
  between operations: 18.7 us -> 1.3 us
  other arithmetic: 14.1 us -> 0 us
    reduce_scatter x2 -> x0, waiting for transfers between devices: 115 us -> none  [the longest x1 65.4 us: per_device(): lax.psum_scatter(input_piece(conv2_weight, back_second), 'mp', scatter_di...]
    all_gather x2 -> x0, waiting for transfers between devices: 79.8 us -> none  [the longest x1 43 us: per_device(): lax.all_gather(features, 'mp', axis=0, tiled=True)]
    pallas_call x0 -> x2, Pallas kernels: none -> 72.3 us  [the longest x1 70.2 us: block_device(): pl.pallas_call(functools.partial(block_kernel, (n_batch, n_mp, channels,...]
    psum x5 -> x0, blocking collectives: 64.1 us -> none  [the longest x1 34.9 us: per_device(): class_logits = lax.psum(partial_logits, 'mp') + head_bias[None, :]]
    another operation x36 -> x0, local copies, waits for them, and re-layouts: 42.7 us -> none  [shifted_taps(): return jnp.stack(pieces)]
    unnamed x138 -> x0, local copies, waits for them, and re-layouts: 37.4 us -> none
    psum x1 -> x0, waiting for transfers between devices: 33.7 us -> none  [per_device(): lax.psum((conv1_grad, conv2_grad, head_grad, head_bias_grad), 'batch')]
    dot_general x9 -> x0, matrix products: 33 us -> none  [the longest x2 14.6 us: weight_piece(): jnp.einsum('on,tcn->otc', grad_low, shifted_taps(piece, 1), preferred_ele...]
  transfers between devices with their start and end apart: 5 -> 0, of which waited for: 5 -> 0; matrix products, arithmetic and copies ran while one was open for 4% -> 0% of each run, Pallas kernels for 0% -> 0%
where the time goes in v1:
time: 73.8 us; the launch traced here: 73.6 us
  Pallas kernels  72.3 us (98%)
  between operations  1.3 us (2%)
    pallas_call x1, Pallas kernels, block_device(): pl.pallas_call(functools.partial(block_kernel, (n_batch, n_mp, channels,...  70.2 us
    pallas_call x1, Pallas kernels, block_device(): pl.pallas_call(finish_kernel, out_shape=(shape((1,), F32), shape((width,...  2.1 us

profile of v1, /device:TPU:0, one launch (start us, length us, event | category | flops | bytes accessed | tf_op | source)
XLA Modules:
  0.0 73.6 jit_solution(10807250919443817752)
XLA Ops:
  1.3 70.2 %shard_map.263 = (f32[32,2048]{1,0:T(8,128)}, f32[9,32,256]{2,1,0:T(8,128)}, f32[9,32,256]{2,1,0:T(8,128)}, f32[48,128]{1,0:T(8,128)}) custom-call(bf16[32,2048]{1,0:T(8,128)(2,1)} %features.1, s32[1]{0:T(128)S(6)} %copy.30.counts, s32[1,32]{1,0:T(1,128)} %bitcast.26, f32[32,100]{1,0:T(8,128)} %teacher.1, bf16[9,32,256]{2,1,0:T(8,128)(2,1)} %bitcast.24, ...), custom_call_target="tpu_custom_call" | custom-call | tf_op jit(solution)/shard_map/pallas_call | solution.py:1116
  71.5 2.1 %shard_map.264 = (f32[1]{0:T(128)}, f32[32,2048]{1,0:T(8,128)}, f32[9,32,256]{2,1,0:T(8,128)}, f32[1,32]{1,0:T(1,128)}, f32[1,32]{1,0:T(1,128)}, /*index=5*/f32[...) custom-call(f32[32,2048]{1,0:T(8,128)} %get-tuple-element.32.feature, ...), custom_call_target="tpu_custom_call" | custom-call | tf_op jit(solution)/shard_map/pallas_call | solution.py:1203

commit v2 on v1

--- a/solution.py
+++ b/solution.py
@@ -365,6 +365,7 @@
         sums_all,
         logit_stage,
         logit_all,
+        head_part,
         field,
         normed1,
         slope1,
@@ -375,10 +376,16 @@
         taps_g,
         raw_x,
         raw_h,
-        layer_x,
-        layer_h,
-        grad_stage,
-        grad_all,
+        strip_taps,
+        live_taps,
+        live_rows,
+        norm_part,
+        norm_edges,
+        live_part,
+        live_edges,
+        columns,
+        strip_stage,
+        strip_all,
         column_part,
         column_stage,
         column_all,
@@ -392,15 +399,15 @@
         send_sem,
         sums_send,
         sums_recv,
-        logit_send,
         logit_recv,
+        head_part_recv,
         cells_recv,
         params_recv,
         counts_recv,
         head_recv,
         weight_recv,
         raw_recv,
-        grad_recv,
+        strip_recv,
         column_recv,
         mean_recv,
         edge_recv,
@@ -419,6 +426,7 @@
     z, y = p // PLANE, p % PLANE
     me = b * n_mp + p
     seat = y * n_batch + b
+    n_seats = PLANE * n_batch
     tall = column_part.shape[2]
     means_end_value = {}
     sent = []
@@ -471,13 +479,6 @@
             taps[lateral, block + cells : 2 * block + cells] = jnp.zeros(
                 (block, channels), BF16
             )
-    for layer in (layer_x, layer_h):
-        for s in range(n_batch * PLANE):
-            for lateral in range(3):
-                layer[s, lateral, 0:block] = jnp.zeros((block, channels), BF16)
-                layer[s, lateral, block + cells : 2 * block + cells] = jnp.zeros(
-                    (block, channels), BF16
-                )
     for load in loads:
         load.wait()
     group = LANES // width
@@ -491,7 +492,13 @@
     params_all[p] = pltpu.roll(own_params, place, 1)
     count = counts[0]
     counts_all[b] = jnp.zeros((8, LANES), F32) + count.astype(F32)
-    head_all[p] = head_here[...]
+    head_all[p] = jnp.concatenate(
+        [
+            head_here[...],
+            jnp.zeros((width, LANES - head_here.shape[1]), BF16),
+        ],
+        axis=1,
+    )
 
     pl.semaphore_wait(barrier, everyone - 1)
 
@@ -502,9 +509,11 @@
         start = (at_z * PLANE + at_y) * width + at_x * strip
         return pl.ds(pl.multiple_of(start, strip), strip)
 
-    far = [lambda v: n_z - 1 - v, lambda v: (v + n_z // 2) % n_z]
-    if n_z == 4:
-        far.append(lambda v: v + 1 - 2 * (v % 2))
+    far = [
+        lambda v: v + 1 - 2 * (v % 2),
+        lambda v: (v + n_z // 2) % n_z,
+        lambda v: n_z - 1 - v,
+    ]
     mates = [(1, 1), (1, 0), (0, 1)]
 
     def column_start(which, weight):
@@ -591,6 +600,7 @@
     for k in range(1, n_mp):
         q = (p + k) % n_mp
         send(features.at[:, cells_of(q)], cells_in.at[p], cells_recv.at[k], b, q)
+    column_start(1, weight2)
     for k in range(1, n_mp):
         q = (p + k) % n_mp
         send(params_all.at[p], params_all.at[p], params_recv.at[k], b, q)
@@ -605,7 +615,6 @@
         )
 
     layer_start(0, weight1)
-    column_start(1, weight2)
     own_cells.wait()
     for k in range(1, n_mp):
         q = (p + n_mp - k) % n_mp
@@ -620,6 +629,8 @@
     store_taps(put_x, by_cell, block)
     raw_x[seat] = by_cell.astype(BF16)
 
+    shard_start(1, weight2)
+    layer_start(1, weight2)
     core_start(0, weight1)
 
     for k in range(1, n_mp):
@@ -732,19 +743,10 @@
             await_bytes(part, raw_recv.at[which, i])
             send(part, part, raw_recv.at[which, 4 + i], x * PLANE + 1 - c, p)
 
-    def raw_end(which, raw, layer):
+    def raw_end(which, raw):
         await_bytes(raw.at[seat_of(0, 0, 1)], raw_recv.at[which, 3])
         for i, (dx, dy) in enumerate(mates):
             await_bytes(raw.at[seat_of(dx, dy, 1)], raw_recv.at[which, 4 + i])
-
-        def build(s, carry):
-            def put(lateral, where, value):
-                layer[s, lateral, where] = value
-
-            store_taps(put, raw[s].astype(F32), block)
-            return carry
-
-        lax.fori_loop(0, n_batch * PLANE, build, 0)
 
     seats = [
         (dx, dy, dc)
@@ -754,11 +756,11 @@
         if dx or dy or dc
     ]
 
-    def grads_start(which, grad):
-        by_row = grad.T
-        for s in range(n_batch * PLANE):
+    def strips_start(which, value):
+        by_row = value.T
+        for s in range(n_seats):
             at_y, at_b = divmod(s, n_batch)
-            grad_stage[which, s] = jnp.concatenate(
+            strip_stage[which, s] = jnp.concatenate(
                 [
                     by_row[start : start + quarter]
                     for start in (
@@ -769,31 +771,106 @@
             ).astype(BF16)
         for i, (dx, dy, dc) in enumerate(seats):
             send(
-                grad_stage.at[which, seat_of(dx, dy, dc)],
-                grad_all.at[which, seat],
-                grad_recv.at[which, i],
+                strip_stage.at[which, seat_of(dx, dy, dc)],
+                strip_all.at[which, seat],
+                strip_recv.at[which, i],
                 ((x + dx) % 2) * PLANE + (c + dc) % 2,
                 z * PLANE + (y + dy) % 2,
             )
-        grad_all[which, seat] = grad_stage[which, seat]
-
-    def grads_end(which, layer):
+        strip_all[which, seat] = strip_stage[which, seat]
+
+    shape = (9, 1, cells)
+    cell = lax.broadcasted_iota(jnp.int32, shape, 2)
+    tap_at = lax.broadcasted_iota(jnp.int32, shape, 0)
+    down = (tap_at >= 3).astype(jnp.int32) + (tap_at >= 6).astype(jnp.int32)
+    from_row = cell // block - down + 1
+    from_column = cell % SIDE - (tap_at - 3 * down) + 1
+    reach = jnp.where(
+        (from_row >= 0)
+        & (from_row < SIDE)
+        & (from_column >= 0)
+        & (from_column < SIDE),
+        1.0,
+        0.0,
+    )
+
+    def moved(value, tap):
+        vertical, lateral = divmod(tap, 3)
+        ahead = (vertical - 1) * block + lateral - 1
+        return (pltpu.roll(value, ahead % cells, 1) if ahead else value) * reach[tap]
+
+    strips = n_z * quarter
+
+    def strips_product(which, raw):
         for i, (dx, dy, dc) in enumerate(seats):
-            await_bytes(grad_all.at[which, seat_of(dx, dy, dc)], grad_recv.at[which, i])
+            await_bytes(
+                strip_all.at[which, seat_of(dx, dy, dc)], strip_recv.at[which, i]
+            )
+        for s in range(n_seats):
+            value = strip_all[which, s].astype(F32)
+            for tap in range(9):
+                strip_taps[
+                    tap * strips : (tap + 1) * strips, s * cells : (s + 1) * cells
+                ] = moved(value, tap).astype(BF16)
+        edges = sum(nn(strip_all[which, s], inside) for s in range(n_seats))
+        return nn(strip_taps[...], raw[...].reshape(-1, channels)), edges
+
+    def live_of(at_y, at_b):
+        lane = lax.broadcasted_iota(jnp.int32, (8, cells), 1)
+        image = (lane // SIDE) % images + (z * PLANE + at_y) * images
+        return (image.astype(F32) < counts_all[at_b][:, 0:1]).astype(F32)
+
+    def norm_product(raw):
+        for s in range(n_seats):
+            alive = live_of(*divmod(s, n_batch))
+            live_rows[s : s + 1] = alive[0:1].astype(F32)
+            for tap in range(9):
+                live_taps[tap : tap + 1, s * cells : (s + 1) * cells] = moved(
+                    alive, tap
+                )[0:1]
+        product, edges = strips_product(2, raw)
+        norm_part[...] = product
+        norm_edges[...] = edges
+        live_part[...] = nn(
+            live_taps[...].astype(BF16), raw[...].reshape(-1, channels)
+        )
+        live_edges[...] = nn(live_rows[...].astype(BF16), inside)
+
+    def own_column(row):
+        columns[...] = jnp.broadcast_to(row, (LANES, channels)).T
+        return jnp.concatenate(
+            [
+                columns[
+                    pl.ds(
+                        pl.multiple_of(
+                            (at_z * PLANE + y) * width + b * quarter, quarter
+                        ),
+                        quarter,
+                    ),
+                    :,
+                ]
+                for at_z in range(n_z)
+            ]
+        )[:, 0:1]
+
+    def column_send(which, product, edges, sums=None):
+        if sums is not None:
+            bias_column, gain_column = (own_column(row / live_cells) for row in sums)
+            edges = edges - (
+                bias_column * row_sum(live_edges[...]) + gain_column * norm_edges[...]
+            )
         mean = means_end(1 - which)
         means_end_value[which] = mean
-        edges = sum(nn(grad_all[which, s], inside) for s in range(n_batch * PLANE))
         for at_z in range(n_z):
             edge_part[which, at_z] = edges[at_z * quarter : (at_z + 1) * quarter]
         for tap in range(9):
-            vertical, lateral = divmod(tap, 3)
-            total = -edges[:, tap : tap + 1] * mean
-            for s in range(n_batch * PLANE):
-                term = nn(
-                    grad_all[which, s],
-                    layer[s, lateral, block * vertical : block * vertical + cells],
+            rows = slice(tap * strips, (tap + 1) * strips)
+            total = product[rows] - edges[:, tap : tap + 1] * mean
+            if sums is not None:
+                total = total - (
+                    bias_column * live_part[tap : tap + 1]
+                    + gain_column * norm_part[rows]
                 )
-                total = total + term
             for at_z in range(n_z):
                 column_part[which, at_z, tap * quarter : (tap + 1) * quarter] = total[
                     at_z * quarter : (at_z + 1) * quarter
@@ -848,6 +925,7 @@
                     tap * quarter : (tap + 1) * quarter
                 ]
 
+    live_taps[...] = jnp.zeros_like(live_taps)
     for which in range(2):
         for at_z in range(n_z):
             column_part[which, at_z, 9 * quarter :] = jnp.zeros(
@@ -859,8 +937,8 @@
     first = conv(taps_x, weight1)
     masked = first * live
     sums_start(0, row_sum(masked), row_sum(masked * first))
-    shard_start(1, weight2)
-    layer_start(1, weight2)
+    raw_start(0, raw_x)
+    core_start(1, weight2)
     total, square = sums_end(0)
     mean1 = total / live_cells
     var1 = square / live_cells - mean1 * mean1
@@ -878,13 +956,14 @@
     store_taps(put_h, hidden, block)
     raw_h[seat] = hidden.astype(BF16)
     means_start(1, hidden)
-    core_start(1, weight2)
     core_end(1, weight2)
 
     second = conv(taps_h, weight2)
     masked = second * live
     sums_start(1, row_sum(masked), row_sum(masked * second))
     raw_start(1, raw_h)
+    strips_start(2, normed1[...] * live)
+    raw_forward(0, raw_x)
     total, square = sums_end(1)
     mean2 = total / live_cells
     var2 = square / live_cells - mean2 * mean2
@@ -899,7 +978,7 @@
     pooled = jnp.sum(pooled.reshape(images, SIDE, channels), axis=1) / float(
         SIDE * SIDE
     )
-    head = head_all[...].reshape(channels, head_all.shape[2]).astype(F32)
+    head = head_all[...].reshape(channels, LANES).astype(F32)[:, 0 : head_here.shape[1]]
     logits = nn(pooled, head, highest) + head_bias_here[...]
     slots = labels_here.shape[1]
     image_at = lax.broadcasted_iota(jnp.int32, (images, slots), 0) + p * images
@@ -923,23 +1002,6 @@
     grad_pre2[...] = pre_grad2
     sums_start(2, row_sum(pre_grad2), row_sum(pre_grad2 * flat2))
 
-    raw_start(0, raw_x)
-    raw_forward(1, raw_h)
-    raw_end(1, raw_h, layer_h)
-
-    bias_grad2, gain_grad2 = sums_end(2)
-    grad_second = (gain2 * rstd2) * (
-        grad_pre2[...]
-        - live * (bias_grad2 + normed2[...] * gain_grad2) / live_cells
-    )
-    grads_start(0, grad_second)
-
-    def put_g(lateral, where, value):
-        taps_g[lateral, where] = value
-
-    store_taps(put_g, grad_second.astype(BF16).astype(F32), block)
-    pre_grad1 = conv_back(taps_g, weight2) * slope1[...]
-    sums_start(3, row_sum(pre_grad1), row_sum(pre_grad1 * normed1[...]))
     classes = logits.shape[1]
     for q in range(n_mp):
         logit_stage[q] = jnp.zeros((2 * images, LANES), F32)
@@ -948,24 +1010,52 @@
         logit_stage[q, images : 2 * images, 0:width] = pooled[
             :, q * width : (q + 1) * width
         ]
-    for to_b, to_p in others:
-        pltpu.make_async_remote_copy(
-            src_ref=logit_stage.at[to_p],
-            dst_ref=logit_all.at[me],
-            send_sem=logit_send,
-            recv_sem=logit_recv,
-            device_id=(to_b, to_p),
-            device_id_type=MESH,
-        ).start()
-    logit_all[me] = logit_stage[p]
-    grads_end(0, layer_h)
-    raw_forward(0, raw_x)
-    raw_end(0, raw_x, layer_x)
+    for k in range(1, n_mp):
+        q = (p + k) % n_mp
+        send(logit_stage.at[q], logit_all.at[p], logit_recv.at[k], b, q)
+    logit_all[p] = logit_stage[p]
+    raw_forward(1, raw_h)
+    raw_end(1, raw_h)
+
+    bias_grad2, gain_grad2 = sums_end(2)
+    grad_second = (gain2 * rstd2) * (
+        grad_pre2[...]
+        - live * (bias_grad2 + normed2[...] * gain_grad2) / live_cells
+    )
+    strips_start(0, grad_second)
+
+    def put_g(lateral, where, value):
+        taps_g[lateral, where] = value
+
+    store_taps(put_g, grad_second.astype(BF16).astype(F32), block)
+    pre_grad1 = conv_back(taps_g, weight2) * slope1[...]
+    sums_start(3, row_sum(pre_grad1), row_sum(pre_grad1 * normed1[...]))
+    scale1 = gain1 * rstd1
+    strips_start(1, scale1 * pre_grad1)
+    product2, edges2 = strips_product(0, raw_h)
+    column_send(0, product2, edges2)
+    for k in range(1, n_mp):
+        await_bytes(logit_all.at[(p + n_mp - k) % n_mp], logit_recv.at[k])
+    both = logit_all[...]
+    upper = lax.broadcasted_iota(jnp.int32, both.shape, 1) < images
+    upper_logits = jnp.where(upper, both, 0.0).reshape(-1, LANES)
+    lifted = jnp.where(upper, pltpu.roll(both, images, 1), 0.0).reshape(-1, LANES)
+    head_part[b, 0:width] = tn(lifted, upper_logits, highest)[0:width]
+    head_part[b, width : width + 8] = jnp.broadcast_to(
+        row_sum(upper_logits), (8, LANES)
+    )
+    for j in range(1, n_batch):
+        part = head_part.at[b]
+        send(part, part, head_part_recv.at[j], (b + j) % n_batch, p)
+    raw_end(0, raw_x)
+    norm_product(raw_x)
+    product1, edges1 = strips_product(1, raw_x)
     bias_grad1, gain_grad1 = sums_end(3)
     grad_first = (gain1 * rstd1) * (
         pre_grad1 - live * (bias_grad1 + normed1[...] * gain_grad1) / live_cells
     )
-    grads_start(1, grad_first)
+    column_send(1, product1, edges1, (scale1 * bias_grad1, scale1 * gain_grad1))
+    quarters_start(0)
     store_taps(put_g, grad_first.astype(BF16).astype(F32), block)
     grad_in = conv_back(taps_g, weight1) + grad_pre2[...]
     cells_stage[...] = (
@@ -975,8 +1065,6 @@
         q = (p + k) % n_mp
         send(cells_stage.at[q], cells_out.at[p], out_recv.at[k], b, q)
     cells_out[p] = cells_stage[p]
-    grads_end(1, layer_x)
-    quarters_start(0)
     quarters_start(1)
 
     def own(row):
@@ -1001,16 +1089,14 @@
     out_small[...] = jnp.zeros_like(out_small)
     for i, row in enumerate(rows):
         out_small[i : i + 1, 0:width] = row
-    await_bytes(logit_all.at[pl.ds(0, everyone - 1)], logit_recv)
-    tall = logit_all[...]
-    upper = lax.broadcasted_iota(jnp.int32, tall.shape, 1) < images
-    upper_logits = jnp.where(upper, tall, 0.0).reshape(-1, LANES)
-    lifted = jnp.where(upper, pltpu.roll(tall, images, 1), 0.0).reshape(-1, LANES)
-    out_small[16 : 16 + width] = tn(lifted, upper_logits, highest)[0:width]
-    columns = row_sum(upper_logits)
-    out_small[8:9] = columns
+    for j in range(1, n_batch):
+        await_bytes(head_part.at[(b + n_batch - j) % n_batch], head_part_recv.at[j])
+    head_sum = sum(head_part[at_b] for at_b in range(n_batch))
+    out_small[16 : 16 + width] = head_sum[0:width]
+    last = head_sum[width : width + 1]
+    out_small[8:9] = last
     out_small[9:10] = jnp.broadcast_to(
-        columns[:, classes : classes + 1] / live_images, (1, LANES)
+        last[:, classes : classes + 1] / live_images, (1, LANES)
     )
 
     quarters_end(0, out_conv2)
@@ -1028,7 +1114,6 @@
             sums_all.at[which, pl.ds(0, everyone - 1), pl.ds(0, 4)],
             sums_send.at[which],
         )
-    await_bytes(logit_all.at[pl.ds(0, everyone - 1)], logit_send)
 
 
 def finish_kernel(
@@ -1134,10 +1219,11 @@
             low(n_mp, width, cells),
             vmem(n_mp, 8, LANES),
             vmem(n_batch, 8, LANES),
-            low(n_mp, width, classes),
+            low(n_mp, width, LANES),
             vmem(4, everyone, 8, LANES),
             vmem(n_mp, 2 * images, LANES),
-            vmem(everyone, 2 * images, LANES),
+            vmem(n_mp, 2 * images, LANES),
+            vmem(n_batch, width + 8, LANES),
             vmem(cells, channels),
             vmem(cells, channels),
             vmem(cells, channels),
@@ -1148,10 +1234,16 @@
             low(3, padded, channels),
             low(seats, cells, channels),
             low(seats, cells, channels),
-            low(seats, 3, padded, channels),
-            low(seats, 3, padded, channels),
-            low(2, seats, n_z * quarter, cells),
-            low(2, seats, n_z * quarter, cells),
+            low(9 * n_z * quarter, seats * cells),
+            vmem(16, seats * cells),
+            vmem(8, cells),
+            vmem(9 * n_z * quarter, channels),
+            vmem(n_z * quarter, LANES),
+            vmem(16, channels),
+            vmem(8, LANES),
+            vmem(channels, LANES),
+            low(3, seats, n_z * quarter, cells),
+            low(3, seats, n_z * quarter, cells),
             vmem(2, n_z, tall, channels),
             low(2, n_z, tall, channels),
             low(2, n_z - 1, tall, channels),
@@ -1162,18 +1254,18 @@
             low(n_mp, width, cells),
             low(n_mp, width, cells),
             dma((14,)),
-            dma((128,)),
+            dma((160,)),
             dma((4,)),
             dma((4,)),
-            dma,
-            dma,
+            dma((n_mp,)),
+            dma((n_batch,)),
             dma((n_mp,)),
             dma((n_mp,)),
             dma((n_batch,)),
             dma((n_mp,)),
             dma((2, 17)),
             dma((2, 7)),
-            dma((2, 7)),
+            dma((3, 7)),
             dma((2, n_z - 1)),
             dma((2, n_z - 1)),
             dma((2, n_z - 1)),

time: 73.8 us -> 68 us (0.921)
  Pallas kernels: 72.3 us -> 66.5 us
    pallas_call x1, Pallas kernels: 70.2 us -> 64.4 us  [block_device(): pl.pallas_call(functools.partial(block_kernel, (n_batch, n_mp, channels,...]
where the time goes in v2:
time: 68 us; the launch traced here: 67.8 us
  Pallas kernels  66.5 us (98%)
  between operations  1.3 us (2%)
    pallas_call x1, Pallas kernels, block_device(): pl.pallas_call(functools.partial(block_kernel, (n_batch, n_mp, channels,...  64.4 us
    pallas_call x1, Pallas kernels, block_device(): pl.pallas_call(finish_kernel, out_shape=(shape((1,), F32), shape((width,...  2.1 us

profile of v2, /device:TPU:0, one launch (start us, length us, event | category | flops | bytes accessed | tf_op | source)
XLA Modules:
  0.0 67.8 jit_solution(8363482659506476125)
XLA Ops:
  1.3 64.4 %shard_map.263 = (f32[32,2048]{1,0:T(8,128)}, f32[9,32,256]{2,1,0:T(8,128)}, f32[9,32,256]{2,1,0:T(8,128)}, f32[48,128]{1,0:T(8,128)}) custom-call(bf16[32,2048]{1,0:T(8,128)(2,1)} %features.1, s32[1]{0:T(128)S(6)} %copy.30.counts, s32[1,32]{1,0:T(1,128)} %bitcast.26, f32[32,100]{1,0:T(8,128)} %teacher.1, bf16[9,32,256]{2,1,0:T(8,128)(2,1)} %bitcast.24, ...), custom_call_target="tpu_custom_call" | custom-call | tf_op jit(solution)/shard_map/pallas_call | solution.py:1201
  65.7 2.1 %shard_map.264 = (f32[1]{0:T(128)}, f32[32,2048]{1,0:T(8,128)}, f32[9,32,256]{2,1,0:T(8,128)}, f32[1,32]{1,0:T(1,128)}, f32[1,32]{1,0:T(1,128)}, /*index=5*/f32[...) custom-call(f32[32,2048]{1,0:T(8,128)} %get-tuple-element.32.feature, ...), custom_call_target="tpu_custom_call" | custom-call | tf_op jit(solution)/shard_map/pallas_call | solution.py:1295

commit v3 on v2

--- a/solution.py
+++ b/solution.py
@@ -347,9 +347,8 @@
 ):
     params, rest = rest[:8], rest[8:]
     (
-        out_features,
-        out_conv1,
-        out_conv2,
+        out_cells,
+        out_quarters,
         out_small,
         weight1,
         weight2,
@@ -427,7 +426,6 @@
     me = b * n_mp + p
     seat = y * n_batch + b
     n_seats = PLANE * n_batch
-    tall = column_part.shape[2]
     means_end_value = {}
     sent = []
 
@@ -446,12 +444,18 @@
     def await_bytes(ref, sem):
         pltpu.make_async_copy(ref, ref, sem).wait()
 
+    far = [
+        lambda v: v + 1 - 2 * (v % 2),
+        lambda v: (v + n_z // 2) % n_z,
+        lambda v: n_z - 1 - v,
+    ]
     others = [
-        ((b + j) % n_batch, (p + k) % n_mp)
-        for k in range(n_mp)
-        for j in range(n_batch)
-        if j or k
-    ]
+        (((x + dx) % 2) * PLANE + (c + dc) % 2, at_z * PLANE + (y + dy) % 2)
+        for at_z in [other(z) for other in reversed(far)] + [z]
+        for dy in (1, 0)
+        for dx in (1, 0)
+        for dc in (1, 0)
+    ][:-1]
 
     loads = [
         (conv1, weight1.at[:, pl.ds(pl.multiple_of(p * width, width), width), :]),
@@ -509,12 +513,7 @@
         start = (at_z * PLANE + at_y) * width + at_x * strip
         return pl.ds(pl.multiple_of(start, strip), strip)
 
-    far = [
-        lambda v: v + 1 - 2 * (v % 2),
-        lambda v: (v + n_z // 2) % n_z,
-        lambda v: n_z - 1 - v,
-    ]
-    mates = [(1, 1), (1, 0), (0, 1)]
+    mates = [(1, 0), (0, 1), (1, 1)]
 
     def column_start(which, weight):
         part = weight.at[:, rows_of(z, y, x), half]
@@ -686,7 +685,7 @@
     def sums_start(which, one, two):
         mine = sums_all.at[which, me, pl.ds(0, 4)]
         sums_all[which, me, 0:4] = jnp.concatenate(halves(one) + halves(two))
-        for to_b, to_p in reversed(others):
+        for to_b, to_p in others:
             pltpu.make_async_remote_copy(
                 src_ref=mine,
                 dst_ref=mine,
@@ -876,7 +875,9 @@
                     at_z * quarter : (at_z + 1) * quarter
                 ]
         for at_z in range(n_z):
-            column_stage[which, at_z] = column_part[which, at_z].astype(BF16)
+            column_stage[which, at_z] = jnp.concatenate(
+                halves(column_part[which, at_z])
+            ).astype(BF16)
         for k, other in enumerate(far):
             send(
                 column_stage.at[which, other(z)],
@@ -893,6 +894,15 @@
                 other(z) * PLANE + y,
             )
 
+    def unfold(piece):
+        return jnp.concatenate(
+            [
+                piece[at : at + 9 * quarter]
+                for at in range(0, piece.shape[0], 9 * quarter)
+            ],
+            axis=1,
+        )
+
     def quarters_start(which):
         for k in range(len(far)):
             await_bytes(column_all.at[which, k], column_recv.at[which, k])
@@ -902,36 +912,22 @@
         total = column_part[which, z]
         for k in range(len(far)):
             edges = edges + edge_all[which, k]
-            total = total + column_all[which, k].astype(F32)
-        back = jnp.concatenate(
-            [edges[:, tap : tap + 1] * mean for tap in range(9)]
-            + [jnp.zeros((tall - 9 * quarter, channels), F32)]
-        )
-        quarter_all[which, b] = (total + back).astype(BF16)
+            total = total + unfold(column_all[which, k].astype(F32))
+        back = jnp.concatenate([edges[:, tap : tap + 1] * mean for tap in range(9)])
+        quarter_all[which, b] = jnp.concatenate(halves(total + back)).astype(BF16)
         for j in range(1, n_batch):
             part = quarter_all.at[which, b]
             send(part, part, quarter_recv.at[which, j], (b + j) % n_batch, p)
 
-    def quarters_end(which, out):
+    def quarters_end(which):
         for j in range(1, n_batch):
             await_bytes(
                 quarter_all.at[which, (b + n_batch - j) % n_batch],
                 quarter_recv.at[which, j],
             )
-        for at_b in range(n_batch):
-            whole = quarter_all[which, at_b].astype(F32)
-            for tap in range(9):
-                out[tap, at_b * quarter : (at_b + 1) * quarter] = whole[
-                    tap * quarter : (tap + 1) * quarter
-                ]
+        out_quarters[which] = quarter_all[which]
 
     live_taps[...] = jnp.zeros_like(live_taps)
-    for which in range(2):
-        for at_z in range(n_z):
-            column_part[which, at_z, 9 * quarter :] = jnp.zeros(
-                (tall - 9 * quarter, channels), F32
-            )
-
     means_start(0, by_cell)
     core_end(0, weight1)
     first = conv(taps_x, weight1)
@@ -1032,8 +1028,25 @@
     sums_start(3, row_sum(pre_grad1), row_sum(pre_grad1 * normed1[...]))
     scale1 = gain1 * rstd1
     strips_start(1, scale1 * pre_grad1)
+    raw_end(0, raw_x)
+    norm_product(raw_x)
     product2, edges2 = strips_product(0, raw_h)
     column_send(0, product2, edges2)
+    product1, edges1 = strips_product(1, raw_x)
+    bias_grad1, gain_grad1 = sums_end(3)
+    grad_first = (gain1 * rstd1) * (
+        pre_grad1 - live * (bias_grad1 + normed1[...] * gain_grad1) / live_cells
+    )
+    column_send(1, product1, edges1, (scale1 * bias_grad1, scale1 * gain_grad1))
+    store_taps(put_g, grad_first.astype(BF16).astype(F32), block)
+    grad_in = conv_back(taps_g, weight1) + grad_pre2[...]
+    cells_stage[...] = (
+        images_first(grad_in, images).T.astype(BF16).reshape(n_mp, width, cells)
+    )
+    for k in range(1, n_mp):
+        q = (p + k) % n_mp
+        send(cells_stage.at[q], cells_out.at[p], out_recv.at[k], b, q)
+    cells_out[p] = cells_stage[p]
     for k in range(1, n_mp):
         await_bytes(logit_all.at[(p + n_mp - k) % n_mp], logit_recv.at[k])
     both = logit_all[...]
@@ -1047,24 +1060,7 @@
     for j in range(1, n_batch):
         part = head_part.at[b]
         send(part, part, head_part_recv.at[j], (b + j) % n_batch, p)
-    raw_end(0, raw_x)
-    norm_product(raw_x)
-    product1, edges1 = strips_product(1, raw_x)
-    bias_grad1, gain_grad1 = sums_end(3)
-    grad_first = (gain1 * rstd1) * (
-        pre_grad1 - live * (bias_grad1 + normed1[...] * gain_grad1) / live_cells
-    )
-    column_send(1, product1, edges1, (scale1 * bias_grad1, scale1 * gain_grad1))
     quarters_start(0)
-    store_taps(put_g, grad_first.astype(BF16).astype(F32), block)
-    grad_in = conv_back(taps_g, weight1) + grad_pre2[...]
-    cells_stage[...] = (
-        images_first(grad_in, images).T.astype(BF16).reshape(n_mp, width, cells)
-    )
-    for k in range(1, n_mp):
-        q = (p + k) % n_mp
-        send(cells_stage.at[q], cells_out.at[p], out_recv.at[k], b, q)
-    cells_out[p] = cells_stage[p]
     quarters_start(1)
 
     def own(row):
@@ -1099,13 +1095,12 @@
         last[:, classes : classes + 1] / live_images, (1, LANES)
     )
 
-    quarters_end(0, out_conv2)
+    quarters_end(0)
     for k in range(1, n_mp):
         q = (p + n_mp - k) % n_mp
         await_bytes(cells_out.at[q], out_recv.at[k])
-    for q in range(n_mp):
-        out_features[:, q * cells : (q + 1) * cells] = cells_out[q].astype(F32)
-    quarters_end(1, out_conv1)
+    out_cells[...] = cells_out[...]
+    quarters_end(1)
 
     for copy in sent:
         copy.wait_send()
@@ -1117,9 +1112,8 @@
 
 
 def finish_kernel(
-    features_in,
-    conv1_in,
-    conv2_in,
+    cells_in,
+    quarters_in,
     small,
     loss,
     features_out,
@@ -1133,9 +1127,19 @@
     head_bias_out,
     *stats_out,
 ):
-    features_out[...] = features_in[...]
-    conv1_out[...] = conv1_in[...]
-    conv2_out[...] = conv2_in[...]
+    n_mp, _, cells = cells_in.shape
+    for q in range(n_mp):
+        features_out[:, q * cells : (q + 1) * cells] = cells_in[q].astype(F32)
+    n_batch = quarters_in.shape[1]
+    quarter = conv1_out.shape[1] // n_batch
+    for which, out in enumerate((conv2_out, conv1_out)):
+        for at_b in range(n_batch):
+            whole = quarters_in[which, at_b].astype(F32)
+            for start in range(0, whole.shape[0], quarter):
+                tap, lanes = start // quarter % 9, start // quarter // 9 * LANES
+                out[
+                    tap, at_b * quarter : (at_b + 1) * quarter, lanes : lanes + LANES
+                ] = whole[start : start + quarter]
     vectors = (gain1_out, bias1_out, gain2_out, bias2_out) + stats_out
     for i, out in enumerate(vectors):
         out[...] = small[i : i + 1, 0 : out.shape[1]]
@@ -1175,7 +1179,7 @@
     quarter = width // n_batch
     seats = n_batch * PLANE
     everyone = n_batch * n_mp
-    tall = -(-9 * quarter // 16) * 16
+    tall = 9 * quarter * (channels // LANES)
     padded = cells + 2 * block
 
     def row(values):
@@ -1201,13 +1205,12 @@
     packed = pl.pallas_call(
         functools.partial(block_kernel, (n_batch, n_mp, channels, images)),
         out_shape=(
-            shape((width, cell_count), F32),
-            shape((9, width, channels), F32),
-            shape((9, width, channels), F32),
+            shape((n_mp, width, cells), BF16),
+            shape((2, n_batch, tall, LANES), BF16),
             shape((16 + width, LANES), F32),
         ),
         in_specs=[any_space, in_smem] + [any_space] * 14,
-        out_specs=(in_vmem,) * 4,
+        out_specs=(in_vmem,) * 3,
         scratch_shapes=[
             low(9, channels, channels),
             low(9, channels, channels),
@@ -1244,13 +1247,13 @@
             vmem(channels, LANES),
             low(3, seats, n_z * quarter, cells),
             low(3, seats, n_z * quarter, cells),
-            vmem(2, n_z, tall, channels),
-            low(2, n_z, tall, channels),
-            low(2, n_z - 1, tall, channels),
+            vmem(2, n_z, 9 * quarter, channels),
+            low(2, n_z, tall, LANES),
+            low(2, n_z - 1, tall, LANES),
             vmem(2, n_z, 8, LANES),
             vmem(2, n_z, quarter, LANES),
             vmem(2, n_z - 1, quarter, LANES),
-            low(2, n_batch, tall, channels),
+            low(2, n_batch, tall, LANES),
             low(n_mp, width, cells),
             low(n_mp, width, cells),
             dma((14,)),
@@ -1310,7 +1313,7 @@
             vector,
             vector,
         ),
-        in_specs=[in_vmem] * 4,
+        in_specs=[in_vmem] * 3,
         out_specs=(in_smem,) + (in_vmem,) * 13,
         compiler_params=pltpu.CompilerParams(vmem_limit_bytes=60 * 2**20),
     )(*packed)

time: 68 us -> 64.3 us (0.946)
  Pallas kernels: 66.5 us -> 62.5 us
    pallas_call x1, Pallas kernels: 64.4 us -> 60.5 us  [block_device(): pl.pallas_call(functools.partial(block_kernel, (n_batch, n_mp, channels,...]
where the time goes in v3:
time: 64.3 us; the launch traced here: 63.8 us
  Pallas kernels  62.5 us (97%)
  between operations  1.3 us (2%)
    pallas_call x1, Pallas kernels, block_device(): pl.pallas_call(functools.partial(block_kernel, (n_batch, n_mp, channels,...  60.5 us
    pallas_call x1, Pallas kernels, block_device(): pl.pallas_call(finish_kernel, out_shape=(shape((1,), F32), shape((width,...  1.99 us

profile of v3, /device:TPU:0, one launch (start us, length us, event | category | flops | bytes accessed | tf_op | source)
XLA Modules:
  0.0 63.8 jit_solution(4483651319080320147)
XLA Ops:
  1.3 60.5 %shard_map.263 = (bf16[8,32,256]{2,1,0:T(8,128)(2,1)}, bf16[2,4,144,128]{3,2,1,0:T(8,128)(2,1)}, f32[48,128]{1,0:T(8,128)}) custom-call(bf16[32,2048]{1,0:T(8,128)(2,1)} %features.1, s32[1]{0:T(128)S(6)} %copy.30.counts, s32[1,32]{1,0:T(1,128)} %bitcast.26, f32[32,100]{1,0:T(8,128)} %teacher.1, bf16[9,32,256]{2,1,0:T(8,128)(2,1)} %bitcast.24, ...), custom_call_target="tpu_custom_call" | custom-call | tf_op jit(solution)/shard_map/pallas_call | solution.py:1205
  61.8 2.0 %shard_map.264 = (f32[1]{0:T(128)}, f32[32,2048]{1,0:T(8,128)}, f32[9,32,256]{2,1,0:T(8,128)}, f32[1,32]{1,0:T(1,128)}, f32[1,32]{1,0:T(1,128)}, /*index=5*/f32[...) custom-call(bf16[8,32,256]{2,1,0:T(8,128)(2,1)} %get-tuple-element.3, ...), custom_call_target="tpu_custom_call" | custom-call | tf_op jit(solution)/shard_map/pallas_call | solution.py:1298

commit v4 on v3

--- a/solution.py
+++ b/solution.py
@@ -820,13 +820,6 @@
         return (image.astype(F32) < counts_all[at_b][:, 0:1]).astype(F32)
 
     def norm_product(raw):
-        for s in range(n_seats):
-            alive = live_of(*divmod(s, n_batch))
-            live_rows[s : s + 1] = alive[0:1].astype(F32)
-            for tap in range(9):
-                live_taps[tap : tap + 1, s * cells : (s + 1) * cells] = moved(
-                    alive, tap
-                )[0:1]
         product, edges = strips_product(2, raw)
         norm_part[...] = product
         norm_edges[...] = edges
@@ -934,6 +927,13 @@
     masked = first * live
     sums_start(0, row_sum(masked), row_sum(masked * first))
     raw_start(0, raw_x)
+    for s in range(n_seats):
+        alive = live_of(*divmod(s, n_batch))
+        live_rows[s : s + 1] = alive[0:1].astype(F32)
+        for tap in range(9):
+            live_taps[tap : tap + 1, s * cells : (s + 1) * cells] = moved(
+                alive, tap
+            )[0:1]
     core_start(1, weight2)
     total, square = sums_end(0)
     mean1 = total / live_cells
@@ -998,6 +998,23 @@
     grad_pre2[...] = pre_grad2
     sums_start(2, row_sum(pre_grad2), row_sum(pre_grad2 * flat2))
 
+    raw_forward(1, raw_h)
+
+    bias_grad2, gain_grad2 = sums_end(2)
+    grad_second = (gain2 * rstd2) * (
+        grad_pre2[...]
+        - live * (bias_grad2 + normed2[...] * gain_grad2) / live_cells
+    )
+    strips_start(0, grad_second)
+
+    def put_g(lateral, where, value):
+        taps_g[lateral, where] = value
+
+    store_taps(put_g, grad_second.astype(BF16).astype(F32), block)
+    pre_grad1 = conv_back(taps_g, weight2) * slope1[...]
+    sums_start(3, row_sum(pre_grad1), row_sum(pre_grad1 * normed1[...]))
+    scale1 = gain1 * rstd1
+    strips_start(1, scale1 * pre_grad1)
     classes = logits.shape[1]
     for q in range(n_mp):
         logit_stage[q] = jnp.zeros((2 * images, LANES), F32)
@@ -1010,26 +1027,9 @@
         q = (p + k) % n_mp
         send(logit_stage.at[q], logit_all.at[p], logit_recv.at[k], b, q)
     logit_all[p] = logit_stage[p]
-    raw_forward(1, raw_h)
-    raw_end(1, raw_h)
-
-    bias_grad2, gain_grad2 = sums_end(2)
-    grad_second = (gain2 * rstd2) * (
-        grad_pre2[...]
-        - live * (bias_grad2 + normed2[...] * gain_grad2) / live_cells
-    )
-    strips_start(0, grad_second)
-
-    def put_g(lateral, where, value):
-        taps_g[lateral, where] = value
-
-    store_taps(put_g, grad_second.astype(BF16).astype(F32), block)
-    pre_grad1 = conv_back(taps_g, weight2) * slope1[...]
-    sums_start(3, row_sum(pre_grad1), row_sum(pre_grad1 * normed1[...]))
-    scale1 = gain1 * rstd1
-    strips_start(1, scale1 * pre_grad1)
     raw_end(0, raw_x)
     norm_product(raw_x)
+    raw_end(1, raw_h)
     product2, edges2 = strips_product(0, raw_h)
     column_send(0, product2, edges2)
     product1, edges1 = strips_product(1, raw_x)

time: 64.3 us -> 63.4 us (0.986)
  no operation moved by 1% of the time
where the time goes in v4:
time: 63.4 us; the launch traced here: 63.3 us
  Pallas kernels  62 us (98%)
  between operations  1.3 us (2%)
    pallas_call x1, Pallas kernels, block_device(): pl.pallas_call(functools.partial(block_kernel, (n_batch, n_mp, channels,...  60 us
    pallas_call x1, Pallas kernels, block_device(): pl.pallas_call(finish_kernel, out_shape=(shape((1,), F32), shape((width,...  1.99 us

profile of v4, /device:TPU:0, one launch (start us, length us, event | category | flops | bytes accessed | tf_op | source)
XLA Modules:
  0.0 63.3 jit_solution(17246705946098798582)
XLA Ops:
  1.3 60.0 %shard_map.263 = (bf16[8,32,256]{2,1,0:T(8,128)(2,1)}, bf16[2,4,144,128]{3,2,1,0:T(8,128)(2,1)}, f32[48,128]{1,0:T(8,128)}) custom-call(bf16[32,2048]{1,0:T(8,128)(2,1)} %features.1, s32[1]{0:T(128)S(6)} %copy.30.counts, s32[1,32]{1,0:T(1,128)} %bitcast.26, f32[32,100]{1,0:T(8,128)} %teacher.1, bf16[9,32,256]{2,1,0:T(8,128)(2,1)} %bitcast.24, ...), custom_call_target="tpu_custom_call" | custom-call | tf_op jit(solution)/shard_map/pallas_call | solution.py:1205
  61.3 2.0 %shard_map.264 = (f32[1]{0:T(128)}, f32[32,2048]{1,0:T(8,128)}, f32[9,32,256]{2,1,0:T(8,128)}, f32[1,32]{1,0:T(1,128)}, f32[1,32]{1,0:T(1,128)}, /*index=5*/f32[...) custom-call(bf16[8,32,256]{2,1,0:T(8,128)(2,1)} %get-tuple-element.3, ...), custom_call_target="tpu_custom_call" | custom-call | tf_op jit(solution)/shard_map/pallas_call | solution.py:1298

commit v5 on v4

--- a/solution.py
+++ b/solution.py
@@ -457,6 +457,12 @@
         for dc in (1, 0)
     ][:-1]
 
+    barrier = pltpu.get_barrier_semaphore()
+    for to_b, to_p in others:
+        pl.semaphore_signal(
+            barrier, inc=1, device_id=(to_b, to_p), device_id_type=MESH
+        )
+
     loads = [
         (conv1, weight1.at[:, pl.ds(pl.multiple_of(p * width, width), width), :]),
         (conv2, weight2.at[:, pl.ds(pl.multiple_of(p * width, width), width), :]),
@@ -471,12 +477,6 @@
     ]
     for load in loads:
         load.start()
-    barrier = pltpu.get_barrier_semaphore()
-    for to_b, to_p in others:
-        pl.semaphore_signal(
-            barrier, inc=1, device_id=(to_b, to_p), device_id_type=MESH
-        )
-
     for taps in (taps_x, taps_h, taps_g):
         for lateral in range(3):
             taps[lateral, 0:block] = jnp.zeros((block, channels), BF16)
@@ -1043,7 +1043,7 @@
     cells_stage[...] = (
         images_first(grad_in, images).T.astype(BF16).reshape(n_mp, width, cells)
     )
-    for k in range(1, n_mp):
+    for k in (4, 5, 3, 6, 2, 7, 1):
         q = (p + k) % n_mp
         send(cells_stage.at[q], cells_out.at[p], out_recv.at[k], b, q)
     cells_out[p] = cells_stage[p]

time: 63.4 us -> 63.3 us (level)
  no operation moved by 1% of the time
where the time goes in v5:
time: 63.3 us; the launch traced here: 63.1 us
  Pallas kernels  61.7 us (97%)
  between operations  1.3 us (2%)
    pallas_call x1, Pallas kernels, block_device(): pl.pallas_call(functools.partial(block_kernel, (n_batch, n_mp, channels,...  59.8 us
    pallas_call x1, Pallas kernels, block_device(): pl.pallas_call(finish_kernel, out_shape=(shape((1,), F32), shape((width,...  1.99 us

profile of v5, /device:TPU:0, one launch (start us, length us, event | category | flops | bytes accessed | tf_op | source)
XLA Modules:
  0.0 63.1 jit_solution(1253193110647807271)
XLA Ops:
  1.3 59.8 %shard_map.263 = (bf16[8,32,256]{2,1,0:T(8,128)(2,1)}, bf16[2,4,144,128]{3,2,1,0:T(8,128)(2,1)}, f32[48,128]{1,0:T(8,128)}) custom-call(bf16[32,2048]{1,0:T(8,128)(2,1)} %features.1, s32[1]{0:T(128)S(6)} %copy.30.counts, s32[1,32]{1,0:T(1,128)} %bitcast.26, f32[32,100]{1,0:T(8,128)} %teacher.1, bf16[9,32,256]{2,1,0:T(8,128)(2,1)} %bitcast.24, ...), custom_call_target="tpu_custom_call" | custom-call | tf_op jit(solution)/shard_map/pallas_call | solution.py:1205
  61.1 2.0 %shard_map.264 = (f32[1]{0:T(128)}, f32[32,2048]{1,0:T(8,128)}, f32[9,32,256]{2,1,0:T(8,128)}, f32[1,32]{1,0:T(1,128)}, f32[1,32]{1,0:T(1,128)}, /*index=5*/f32[...) custom-call(bf16[8,32,256]{2,1,0:T(8,128)(2,1)} %get-tuple-element.3, ...), custom_call_target="tpu_custom_call" | custom-call | tf_op jit(solution)/shard_map/pallas_call | solution.py:1298
